TPU v7x, 32 devices: a whole 2x2x4 slice. The times are simulated.
32 devices in a mesh: seq: 16 (over z, y, core), mp: 2 (over x).
Axes of the slice: x: 2, y: 2, z: 4, core: 2. Of those that a mesh axis runs over, the one named last changes fastest.
Arguments:
- tokens: bfloat16 [4096, 1024], P(('seq', 'mp')), may hold values from -6 to 6
- positions: int32 [4096], P('seq'), may hold values from 0 to 1023, as said below
- counts: int32 [16], P('seq'), may hold values from 128 to 256, as said below
- cotangent: bfloat16 [4096, 1024], P(('seq', 'mp')), may hold values from -6 to 6
- gains: bfloat16 [2, 1024], P(None, ('seq', 'mp')), may hold values from 0.5 to 1.5
- in_w: bfloat16 [1024, 3, 1024], P('seq', None, 'mp'), may hold values from -0.1875 to 0.1875
- out_w: bfloat16 [1024, 1024], P('mp', 'seq'), may hold values from -0.1875 to 0.1875
- gate_up: bfloat16 [1024, 2, 4608], P('seq', None, 'mp'), may hold values from -0.1875 to 0.1875
- down_w: bfloat16 [4608, 1024], P('mp', 'seq'), may hold values from -0.09375 to 0.09375
- conv_w: bfloat16 [3, 1024], P(None, ('mp', 'seq')), may hold values from -3 to 3
Outputs:
- mixed: bfloat16 [4096, 1024], P(('seq', 'mp'))
- grad_input: bfloat16 [4096, 1024], P(('seq', 'mp'))
- grad_gains: float32 [2, 1024], P(None, ('seq', 'mp'))
- grad_in_w: float32 [1024, 3, 1024], P('seq', None, 'mp')
- grad_out_w: float32 [1024, 1024], P('mp', 'seq')
- grad_gate_up: float32 [1024, 2, 4608], P('seq', None, 'mp')
- grad_down_w: float32 [4608, 1024], P('mp', 'seq')
- grad_conv_w: float32 [3, 1024], P(None, ('mp', 'seq'))
Inputs may be any that keep to these rules, and one draw needn't show every extreme that they name: `counts`: each seq shard's valid rows come first; one shard has 256 valid rows and one has 128. `positions`: on valid rows, the position counts tokens since the document's first token along the token stream; 0 marks a document start and every invalid row. A document has at most 1024 tokens.
All inputs are finite; a program needn't handle non-finite values.
Results may differ from a plain program's by a relative error of at most 0.019.
Values may be sent and summed in bfloat16 or wider, within the bound.
A program may use at most 128 MiB of HBM per device.

v0:
```python
import jax
import jax.numpy as jnp
from jax import lax
from jax.sharding import PartitionSpec as P

eps = 1e-05


def from_behind(value, axis, steps):
    count = lax.axis_size(axis)
    leading, last = (max(0, -steps), min(count, count - steps))
    return lax.ppermute(value, axis, [(source, source + steps) for source in range(leading, last)])


def contract_rows(left, right):
    return lax.dot_general(
        left, right, (((0,), (0,)), ((), ())), preferred_element_type=jnp.float32
    )


def contract_cols(left, right):
    return lax.dot_general(
        left, right, (((1,), (1,)), ((), ())), preferred_element_type=jnp.float32
    )


def norm_scale(values):
    return lax.rsqrt(jnp.mean(values * values, axis=-1, keepdims=True) + eps)


def norm_back(values, scale, gain, grad):
    weighted = grad * gain
    cubed = scale * scale * scale
    return scale * weighted - values * cubed * jnp.mean(weighted * values, axis=-1, keepdims=True)


def on_device(tokens, positions, counts, cotangent, gains, in_w, out_w, gate_up, down_w, conv_w):
    rows, width = tokens.shape
    group = positions.shape[0]
    count = counts[0]
    mp_place = lax.axis_index("mp")
    w_in, w_out, w_gu, w_down, w_conv = (
        lax.all_gather(in_w, "seq", axis=0, tiled=True),
        lax.all_gather(out_w, "seq", axis=1, tiled=True),
        lax.all_gather(gate_up, "seq", axis=0, tiled=True),
        lax.all_gather(down_w, "seq", axis=1, tiled=True),
        lax.all_gather(conv_w, "seq", axis=1, tiled=True),
    )
    gain_all = lax.all_gather(gains, ("seq", "mp"), axis=1, tiled=True).astype(jnp.float32)
    chans = w_in.shape[2]
    units = w_gu.shape[2]
    in_flat = w_in.reshape(width, 3 * chans)
    gu_flat = w_gu.reshape(width, 2 * units)
    conv_taps = w_conv.astype(jnp.float32)
    own_rows = mp_place * rows + jnp.arange(rows, dtype=jnp.int32)
    own_valid = (own_rows < count)[:, None]
    inputs = tokens.astype(jnp.float32)
    scale_one = norm_scale(inputs)
    normed_one = (inputs * scale_one * gain_all[0]).astype(jnp.bfloat16)
    mixer_all = lax.all_gather(normed_one, "mp", axis=0, tiled=True)
    proj = jnp.dot(mixer_all, in_flat, preferred_element_type=jnp.float32)
    bgate = proj[:, :chans]
    cgate = proj[:, chans : 2 * chans]
    xin = proj[:, 2 * chans :]
    gated = (bgate * xin).astype(jnp.bfloat16)
    tail = lax.dynamic_slice_in_dim(gated, count - 2, 2, 0)
    before = from_behind(tail, "seq", 1)
    extended = jnp.concatenate([before, gated], axis=0).astype(jnp.float32)
    one_back = extended[1 : group + 1]
    two_back = extended[:group]
    keep_one = (positions >= 1).astype(jnp.float32)[:, None]
    keep_two = (positions >= 2).astype(jnp.float32)[:, None]
    current = gated.astype(jnp.float32)
    conv = (
        conv_taps[2] * current
        + keep_one * conv_taps[1] * one_back
        + keep_two * conv_taps[0] * two_back
    )
    mixed_in = (cgate * conv).astype(jnp.bfloat16)
    out_part = jnp.dot(mixed_in, w_out, preferred_element_type=jnp.float32)
    resid = inputs + lax.psum_scatter(out_part, "mp", scatter_dimension=0, tiled=True)
    scale_two = norm_scale(resid)
    normed_two = (resid * scale_two * gain_all[1]).astype(jnp.bfloat16)
    grad_out = jnp.where(own_valid, cotangent, jnp.zeros_like(cotangent))
    ff_all, grad_all = (
        lax.all_gather(normed_two, "mp", axis=0, tiled=True),
        lax.all_gather(grad_out, "mp", axis=0, tiled=True),
    )
    both = jnp.dot(ff_all, gu_flat, preferred_element_type=jnp.float32)
    gate = both[:, :units]
    upper = both[:, units:]
    sigma = jax.nn.sigmoid(gate)
    active = gate * sigma
    hidden = (active * upper).astype(jnp.bfloat16)
    ff_part = jnp.dot(hidden, w_down, preferred_element_type=jnp.float32)
    final = resid + lax.psum_scatter(
        ff_part.astype(jnp.bfloat16), "mp", scatter_dimension=0, tiled=True
    ).astype(jnp.float32)
    mixed = jnp.where(own_valid, final, jnp.zeros_like(final)).astype(jnp.bfloat16)
    w_in, w_out, w_gu, w_down, w_conv = (
        lax.all_gather(in_w, "seq", axis=0, tiled=True),
        lax.all_gather(out_w, "seq", axis=1, tiled=True),
        lax.all_gather(gate_up, "seq", axis=0, tiled=True),
        lax.all_gather(down_w, "seq", axis=1, tiled=True),
        lax.all_gather(conv_w, "seq", axis=1, tiled=True),
    )
    in_flat = w_in.reshape(width, 3 * chans)
    gu_flat = w_gu.reshape(width, 2 * units)
    conv_taps = w_conv.astype(jnp.float32)
    grad_hidden = contract_cols(grad_all, w_down)
    slope = sigma * (1.0 + gate * (1.0 - sigma))
    grad_both = jnp.concatenate([grad_hidden * upper * slope, grad_hidden * active], axis=1).astype(
        jnp.bfloat16
    )
    term_down = contract_rows(hidden, grad_all)
    term_gu = contract_rows(ff_all, grad_both).reshape(width, 2, units)
    back_two = lax.psum_scatter(
        contract_cols(grad_both, gu_flat), "mp", scatter_dimension=0, tiled=True
    )
    grad_resid = grad_out.astype(jnp.float32) + norm_back(resid, scale_two, gain_all[1], back_two)
    gain_two = jnp.sum(back_two * resid * scale_two, axis=0)
    grad_o_all = lax.all_gather(grad_resid.astype(jnp.bfloat16), "mp", axis=0, tiled=True)
    term_out = contract_rows(mixed_in, grad_o_all)
    grad_mix = contract_cols(grad_o_all, w_out)
    grad_cgate = grad_mix * conv
    grad_conv = grad_mix * cgate
    lead_one = keep_one * grad_conv
    lead_two = keep_two * grad_conv
    head = jnp.stack(
        [conv_taps[0] * lead_two[0], conv_taps[1] * lead_one[0] + conv_taps[0] * lead_two[1]]
    )
    after = from_behind(head, "seq", -1)
    zero_one = jnp.zeros((1, chans), jnp.float32)
    zero_two = jnp.zeros((2, chans), jnp.float32)
    grad_gated = (
        conv_taps[2] * grad_conv
        + conv_taps[1] * jnp.concatenate([lead_one[1:], zero_one], axis=0)
        + conv_taps[0] * jnp.concatenate([lead_two[2:], zero_two], axis=0)
    )
    border = lax.dynamic_slice_in_dim(grad_gated, count - 2, 2, 0)
    grad_gated = lax.dynamic_update_slice_in_dim(grad_gated, border + after, count - 2, 0)
    term_conv = jnp.stack(
        [
            jnp.sum(lead_two * two_back, axis=0),
            jnp.sum(lead_one * one_back, axis=0),
            jnp.sum(grad_conv * current, axis=0),
        ]
    )
    grad_proj = jnp.concatenate([grad_gated * xin, grad_cgate, grad_gated * bgate], axis=1).astype(
        jnp.bfloat16
    )
    term_in = contract_rows(mixer_all, grad_proj).reshape(width, 3, chans)
    back_one = lax.psum_scatter(
        contract_cols(grad_proj, in_flat).astype(jnp.bfloat16),
        "mp",
        scatter_dimension=0,
        tiled=True,
    ).astype(jnp.float32)
    grad_input = (grad_resid + norm_back(inputs, scale_one, gain_all[0], back_one)).astype(
        jnp.bfloat16
    )
    gain_one = jnp.sum(back_one * inputs * scale_one, axis=0)
    grad_gains = lax.psum_scatter(
        jnp.stack([gain_one, gain_two]), ("seq", "mp"), scatter_dimension=1, tiled=True
    )
    summed = (
        lax.psum_scatter(
            term_in.astype(jnp.bfloat16), "seq", scatter_dimension=0, tiled=True
        ).astype(jnp.float32),
        lax.psum_scatter(
            term_out.astype(jnp.bfloat16), "seq", scatter_dimension=1, tiled=True
        ).astype(jnp.float32),
        lax.psum_scatter(
            term_gu.astype(jnp.bfloat16), "seq", scatter_dimension=0, tiled=True
        ).astype(jnp.float32),
        lax.psum_scatter(
            term_down.astype(jnp.bfloat16), "seq", scatter_dimension=1, tiled=True
        ).astype(jnp.float32),
        lax.psum_scatter(
            term_conv.astype(jnp.bfloat16), "seq", scatter_dimension=1, tiled=True
        ).astype(jnp.float32),
    )
    return (mixed, grad_input, grad_gains, summed[0], summed[1], summed[2], summed[3], summed[4])


def solution(mesh):
    placed = (
        P(("seq", "mp"), None),
        P("seq"),
        P("seq"),
        P(("seq", "mp"), None),
        P(None, ("seq", "mp")),
        P("seq", None, "mp"),
        P("mp", "seq"),
        P("seq", None, "mp"),
        P("mp", "seq"),
        P(None, ("mp", "seq")),
    )
    return jax.shard_map(
        on_device,
        mesh=mesh,
        in_specs=placed,
        out_specs=(
            P(("seq", "mp"), None),
            P(("seq", "mp"), None),
            P(None, ("seq", "mp")),
            P("seq", None, "mp"),
            P("mp", "seq"),
            P("seq", None, "mp"),
            P("mp", "seq"),
            P(None, ("mp", "seq")),
        ),
        check_vma=False,
    )
```

profile of v0, /device:TPU:0, one launch (start us, length us, event | category | flops | bytes accessed | tf_op | source)
XLA Modules:
  0.0 959.5 jit_solution(15589934328804069246)
XLA Ops:
  8.7 69.6 %all-gather = bf16[32,32,2]{1,2,0:T(2,128)(2,1)S(1)} all-gather(bf16[1,32,2]{1,2,0:T(2,128)(2,1)} %bitcast.83), channel_id=1, replica_groups=mesh['seq'=16,'mp'=2] {'seq','mp'}, dimensions={0}, use_global_device_ids=true | all-gather | bytes 4224 | tf_op jit(solution)/shard_map/all_gather | solution.py:49
  79.5 17.4 %all-gather.1 = bf16[16,32,3]{1,2,0:T(4,128)(2,1)S(1)} all-gather(bf16[1,32,3]{1,2,0:T(4,128)(2,1)} %bitcast.82), channel_id=1, replica_groups=mesh['seq'=16,'mp'=2] {'seq'}, dimensions={0}, use_global_device_ids=true | all-gather | bytes 3264 | tf_op jit(solution)/shard_map/all_gather | solution.py:47
  98.8 9.2 all_gather.36
  108.1 4.9 copy.32
  112.9 2.9 fusion.24
  118.6 2.8 fusion.25
  122.7 9.5 all_gather.43
  132.3 12.7 %reduce-scatter.13.cloned.1.call-done = f32[128,1024]{1,0:T(8,128)} async-done(((f32[256,1024]{1,0:T(8,128)}), f32[128,1024]{1,0:T(8,128)}) %reduce-scatter.13.cloned.1.call-update) | async-done | bytes 524304 | tf_op jit(solution)/shard_map/reduce_scatter | solution.py:81
  146.3 9.1 all_gather.40
  155.3 71.3 %all-gather.11.cloned.1.call-done = bf16[1024,2,2304]{2,1,0:T(2,128)(2,1)} async-done(((bf16[64,2,2304]{2,1,0:T(2,128)(2,1)}), bf16[1024,2,2304]{2,1,0:T(2,128)(2,1)}) %all-gather.11.cloned.1.call-update) | async-done | bytes 9437200 | tf_op jit(solution)/shard_map/all_gather | solution.py:45
  226.6 9.0 copy.41
  235.6 8.6 fusion.26
  244.2 36.3 %all-gather.13.cloned.1.call-done = bf16[2304,1024]{0,1:T(8,128)(2,1)} async-done(((bf16[2304,64]{0,1:T(8,128)(2,1)}), bf16[2304,1024]{0,1:T(8,128)(2,1)}) %all-gather.13.cloned.1.call-update) | async-done | bytes 4718608 | tf_op jit(solution)/shard_map/all_gather | solution.py:46
  280.6 6.9 multiply_convert_fusion.1
  288.9 3.6 fusion.1
  292.6 4.9 convolution_convert_fusion.4
  297.8 13.8 %reduce-scatter.17.cloned.1.call-done = f32[128,1024]{1,0:T(8,128)} async-done(((f32[256,1024]{1,0:T(8,128)}), f32[128,1024]{1,0:T(8,128)}) %reduce-scatter.17.cloned.1.call-update) | async-done | bytes 524304 | tf_op jit(solution)/shard_map/reduce_scatter | solution.py:117
  312.8 16.2 %reduce-scatter.15.cloned.1.call-done = bf16[128,1024]{1,0:T(8,128)(2,1)} async-done(((bf16[256,1024]{1,0:T(8,128)(2,1)}), bf16[128,1024]{1,0:T(8,128)(2,1)}) %reduce-scatter.15.cloned.1.call-update) | async-done | bytes 262160 | tf_op jit(solution)/shard_map/reduce_scatter | solution.py:96
  331.4 8.7 all_gather.44
  345.1 3.9 convolution_convert_fusion.5
  350.0 14.1 %reduce-scatter.19.cloned.1.call-done = bf16[128,1024]{1,0:T(8,128)(2,1)} async-done(((bf16[256,1024]{1,0:T(8,128)(2,1)}), bf16[128,1024]{1,0:T(8,128)(2,1)}) %reduce-scatter.19.cloned.1.call-update) | async-done | bytes 262160 | tf_op jit(solution)/shard_map/reduce_scatter | solution.py:153
  368.0 3.6 convolution_convert_fusion.1
  373.5 5.1 convolution_convert_fusion
  378.6 13.1 %convert_element_type.123 = bf16[1024,2,2304]{2,1,0:T(2,128)(2,1)} reshape(bf16[1024,4608]{1,0:T(8,128)(2,1)} %convolution_convert_fusion) | data formatting | bytes 18874368 | tf_op jit(solution)/shard_map/convert_element_type | solution.py:174
  391.8 2.7 convolution_convert_fusion.2
  394.5 3.2 copy.34
  397.6 5.7 copy.35
  405.3 18.0 %reduce-scatter.27.cloned.1.call-done = bf16[32,3]{1,0:T(8,128)(2,1)} async-done(((bf16[512,3]{1,0:T(8,128)(2,1)}), bf16[32,3]{1,0:T(8,128)(2,1)}) %reduce-scatter.27.cloned.1.call-update) | async-done | bytes 208
  425.6 132.9 %reduce-scatter.25.cloned.1.call-done = f32[32,2]{1,0:T(8,128)} async-done(((f32[1024,2]{1,0:T(8,128)}), f32[32,2]{1,0:T(8,128)}) %reduce-scatter.25.cloned.1.call-update) | async-done | bytes 272
  559.9 56.0 %reduce-scatter.21.cloned.1.call-done = bf16[512,64]{0,1:T(8,128)(2,1)} async-done(((bf16[512,1024]{0,1:T(8,128)(2,1)}), bf16[512,64]{0,1:T(8,128)(2,1)}) %reduce-scatter.21.cloned.1.call-update) | async-done | bytes 65552 | tf_op jit(solution)/shard_map/reduce_scatter | solution.py:170
  617.3 76.8 %reduce-scatter.23.cloned.1.call-done = bf16[2304,64]{0,1:T(8,128)(2,1)} async-done(((bf16[2304,1024]{0,1:T(8,128)(2,1)}), bf16[2304,64]{0,1:T(8,128)(2,1)}) %reduce-scatter.23.cloned.1.call-update) | async-done | bytes 294928 | tf_op jit(solution)/shard_map/reduce_scatter | solution.py:176
  696.0 252.7 %all-reduce.7.cloned.1.call-done = (bf16[1024,3,512]{2,1,0:T(4,128)(2,1)}, bf16[1024,2,2304]{2,1,0:T(2,128)(2,1)}) async-done(((bf16[1024,3,512]{2,1,0:T(4,128)(2,1)}, bf16[1024,2,2304]{2,1,0:T(2,128)(2,1)}), (bf16[1024,3,512]{2,1,0:T(4,128)(2,1)}, bf16[1024,2,2304]{2,1,0:T(2,128)(2,1)})) %all-reduce.7.cloned.1.call-update) | async-done | bytes 12582928
  (127 shorter events, 38.5 us)
Async XLA Ops:
  7.2 100.9 %all-gather.7.cloned.1.call-start = ((), (), s32[]{:S(2)}) async-start(), calls=%async_computation.8 | async-start | bytes 3342336 | tf_op jit(solution)/shard_map/all_gather | solution.py:43
  7.9 110.7 %all-gather.9.cloned.1.call-start = ((), (), s32[]{:S(2)}) async-start(), calls=%async_computation.9 | async-start | bytes 1114112 | tf_op jit(solution)/shard_map/all_gather | solution.py:44
  8.7 136.3 %reduce-scatter.13.cloned.1.call-start = ((), (), s32[]{:S(2)}) async-start(), calls=%async_computation.10 | async-start | bytes 1572864 | tf_op jit(solution)/shard_map/reduce_scatter | solution.py:81
  108.0 4.9 copy-start.7
  112.9 4.5 copy-start.20
  116.0 2.2 collective-permute-start
  118.5 4.2 copy-start.5
  118.5 4.1 copy-start.15
  118.5 26.4 %copy-start.1 = (bf16[128,1024]{1,0:T(8,128)(2,1)S(1)}, bf16[128,1024]{1,0:T(8,128)(2,1)}, u32[]{:S(2)}) copy-start(bf16[128,1024]{1,0:T(8,128)(2,1)} %param.10) | copy-start | bytes 786436
  121.4 105.2 %all-gather.11.cloned.1.call-start = ((), (), s32[]{:S(2)}) async-start(), calls=%async_computation.11 | async-start | bytes 10027008 | tf_op jit(solution)/shard_map/all_gather | solution.py:45
  122.0 158.6 %all-gather.13.cloned.1.call-start = ((), (), s32[]{:S(2)}) async-start(), calls=%async_computation.12 | async-start | bytes 5013504 | tf_op jit(solution)/shard_map/all_gather | solution.py:46
  122.6 189.0 %reduce-scatter.17.cloned.1.call-start = ((), (), s32[]{:S(2)}) async-start(), calls=%async_computation.14 | async-start | bytes 1572864 | tf_op jit(solution)/shard_map/reduce_scatter | solution.py:117
  280.6 8.3 copy-start
  292.6 36.4 %reduce-scatter.15.cloned.1.call-start = ((), (), s32[]{:S(2)}) async-start(), calls=%async_computation.13 | async-start | bytes 786432 | tf_op jit(solution)/shard_map/reduce_scatter | solution.py:96
  297.5 66.6 %reduce-scatter.19.cloned.1.call-start = ((), (), s32[]{:S(2)}) async-start(), calls=%async_computation.15 | async-start | bytes 786432 | tf_op jit(solution)/shard_map/reduce_scatter | solution.py:153
  329.0 11.2 %copy-start.3 = (bf16[512,1024]{0,1:T(8,128)(2,1)S(1)}, bf16[512,1024]{0,1:T(8,128)(2,1)}, u32[]{:S(2)}) copy-start(bf16[512,1024]{0,1:T(8,128)(2,1)} %all-gather.9.cloned.1.call-done) | copy-start | bytes 3145732
  341.6 3.1 collective-permute-start.1
  345.1 3.9 copy-start.18
  349.0 17.5 %copy-start.6 = (bf16[256,512]{1,0:T(8,128)(2,1)S(1)}, bf16[256,512]{1,0:T(8,128)(2,1)}, u32[]{:S(2)}) copy-start(bf16[256,512]{1,0:T(8,128)(2,1)} %copy-done.5) | copy-start | bytes 786436
  349.0 74.3 %reduce-scatter.27.cloned.1.call-start = ((), (), s32[]{:S(2)}) async-start(), calls=%async_computation.19 | async-start | bytes 139264
  349.1 18.9 %copy-start.4 = (bf16[256,2304]{1,0:T(8,128)(2,1)S(1)}, bf16[256,2304]{1,0:T(8,128)(2,1)}, u32[]{:S(2)}) copy-start(bf16[256,2304]{1,0:T(8,128)(2,1)} %get-tuple-element.49) | copy-start | bytes 3538948
  349.1 18.9 %copy-start.9 = (bf16[256,1024]{1,0:T(8,128)(2,1)S(1)}, bf16[256,1024]{1,0:T(8,128)(2,1)}, u32[]{:S(2)}) copy-start(bf16[256,1024]{1,0:T(8,128)(2,1)} %all_gather.43) | copy-start | bytes 1572868
  350.0 208.5 %reduce-scatter.25.cloned.1.call-start = ((), (), s32[]{:S(2)}) async-start(), calls=%async_computation.18 | async-start | bytes 540672
  366.4 249.4 %reduce-scatter.21.cloned.1.call-start = ((), (), s32[]{:S(2)}) async-start(), calls=%async_computation.16 | async-start | bytes 1114112 | tf_op jit(solution)/shard_map/reduce_scatter | solution.py:170
  368.0 326.2 %reduce-scatter.23.cloned.1.call-start = ((), (), s32[]{:S(2)}) async-start(), calls=%async_computation.17 | async-start | bytes 5013504 | tf_op jit(solution)/shard_map/reduce_scatter | solution.py:176
  371.7 1.8 copy-start.14
  371.7 577.0 %all-reduce.7.cloned.1.call-start = ((), (), s32[]{:S(2)}) async-start(), calls=%async_computation.20 | async-start | bytes 27262976
  378.6 13.2 %copy-start.8 = (bf16[256,1024]{1,0:T(8,128)(2,1)S(1)}, bf16[256,1024]{1,0:T(8,128)(2,1)}, u32[]{:S(2)}) copy-start(bf16[256,1024]{1,0:T(8,128)(2,1)} %copy-done.7) | copy-start | bytes 1572868
  378.6 13.2 %copy-start.17 = (bf16[256,512]{1,0:T(8,128)(2,1)S(1)}, bf16[256,512]{1,0:T(8,128)(2,1)}, u32[]{:S(2)}) copy-start(bf16[256,512]{1,0:T(8,128)(2,1)} %get-tuple-element.52) | copy-start | bytes 786436
  378.6 13.2 %copy-start.19 = (bf16[256,512]{1,0:T(8,128)(2,1)S(1)}, bf16[256,512]{1,0:T(8,128)(2,1)}, u32[]{:S(2)}) copy-start(bf16[256,512]{1,0:T(8,128)(2,1)} %copy-done.18) | copy-start | bytes 786436
  403.4 21.3 %copy-start.10 = (f32[128,1024]{1,0:T(8,128)S(1)}, f32[128,1024]{1,0:T(8,128)}, u32[]{:S(2)}) copy-start(f32[128,1024]{1,0:T(8,128)} %get-tuple-element.44) | copy-start | bytes 1572868
  403.4 21.3 %copy-start.16 = (bf16[128,1024]{1,0:T(8,128)(2,1)S(1)}, bf16[128,1024]{1,0:T(8,128)(2,1)}, u32[]{:S(2)}) copy-start(bf16[128,1024]{1,0:T(8,128)(2,1)} %reduce-scatter.19.cloned.1.call-done) | copy-start | bytes 786436
  (5 other events, 5.5 us)
Sparse Core Ops, SparseCore 0:
  10.2 47.9 all-gather.6
  60.3 36.6 all-gather.8
  121.5 23.3 reduce-scatter.12
  147.3 79.2 all-gather.10
  229.0 51.5 all-gather.12
  292.7 18.8 reduce-scatter.16
  314.4 14.5 reduce-scatter.14
  349.1 14.9 reduce-scatter.18
  368.2 55.0 reduce-scatter.26
  425.4 133.0 reduce-scatter.24
  562.6 53.2 reduce-scatter.20
  619.5 74.5 reduce-scatter.22
  698.9 249.7 all-reduce.6
where the time goes:
time: 961 us; the launch traced here: 960 us
  waiting for transfers between devices  706 us (73%)
  blocking collectives  124 us (13%)
  matrix products  47.9 us (5%)
  local copies, waits for them, and re-layouts  45.7 us (5%)
  other arithmetic  17.7 us (2%)
  between operations  15.6 us (2%)
    unnamed x16, waiting for transfers between devices  406 us
    reduce_scatter x1, waiting for transfers between devices, on_device(): lax.psum_scatter(term_down.astype(jnp.bfloat16), 'seq', scatter_dimension...  76.8 us
    all_gather x1, waiting for transfers between devices, on_device(): lax.all_gather(gate_up, 'seq', axis=0, tiled=True)  71.3 us
    all_gather x1, blocking collectives, on_device(): lax.all_gather(gains, ('seq', 'mp'), axis=1, tiled=True).astype(jnp.float32)  69.6 us
    reduce_scatter x1, waiting for transfers between devices, on_device(): lax.psum_scatter(term_out.astype(jnp.bfloat16), 'seq', scatter_dimension=...  56 us
    all_gather x1, waiting for transfers between devices, on_device(): lax.all_gather(down_w, 'seq', axis=1, tiled=True)  36.3 us
  transfers between devices with their start and end apart: 15, of which 13 were waited for; matrix products, arithmetic and copies ran while one was open for 9% of the time, Pallas kernels for 0%

commit v1 on v0

v1 whole, which is shorter than its diff:
```python
import functools

import jax
import jax.numpy as jnp
from jax import lax
from jax.experimental import pallas as pl
from jax.experimental.pallas import tpu as pltpu
from jax.sharding import PartitionSpec as P

eps = 1e-05
MESH = pl.DeviceIdType.MESH
DEPTH = 4
CORES = 2
LANES = 128
VMEM_BYTES = 58 * 1024 * 1024


def contract_rows(left, right):
    return lax.dot_general(
        left, right, (((0,), (0,)), ((), ())), preferred_element_type=jnp.float32
    )


def contract_cols(left, right):
    return lax.dot_general(
        left, right, (((1,), (1,)), ((), ())), preferred_element_type=jnp.float32
    )


def norm_scale(values):
    return lax.rsqrt(jnp.mean(values * values, axis=-1, keepdims=True) + eps)


def norm_back(values, scale, gain, grad):
    weighted = grad * gain
    cubed = scale * scale * scale
    return scale * weighted - values * cubed * jnp.mean(weighted * values, axis=-1, keepdims=True)


def from_behind(value, axis, steps):
    count = lax.axis_size(axis)
    leading, last = (max(0, -steps), min(count, count - steps))
    return lax.ppermute(value, axis, [(source, source + steps) for source in range(leading, last)])


def pieces_of(widths, size):
    pieces = []
    for place, width in enumerate(widths):
        step = size if width % size == 0 else width
        pieces.extend((place, start, step) for start in range(0, width, step))
    return pieces


def seq_place(tall):
    here = lax.axis_index("seq")
    core = lax.rem(here, CORES)
    chip = here // CORES
    return chip // tall, lax.rem(chip, tall), core


def seq_index(tall, z, y, core):
    return (z * tall + y) * CORES + core


def greet(partners):
    barrier = pltpu.get_barrier_semaphore()
    for partner in partners:
        pl.semaphore_signal(barrier, inc=1, device_id=partner, device_id_type=MESH)
    pl.semaphore_wait(barrier, len(partners))


def remote(source, target, send, recv, partner):
    return pltpu.make_async_remote_copy(
        src_ref=source,
        dst_ref=target,
        send_sem=send,
        recv_sem=recv,
        device_id=partner,
        device_id_type=MESH,
    )


def gather_kernel(pieces, arrays, halves, tall, wide, *refs):
    ins = refs[:arrays]
    rows_in = refs[arrays : arrays + halves]
    outs = refs[arrays + halves : 2 * arrays + halves]
    rows_out = refs[2 * arrays + halves : 2 * (arrays + halves)]
    (own_sem, z_send, z_recv, y_send, y_recv, c_send, c_recv, x_send, x_recv) = refs[
        2 * (arrays + halves) :
    ]
    z, y, core = seq_place(tall)
    part = lax.axis_index("mp")

    def at_z(step):
        return lax.rem(z + step + DEPTH, DEPTH)

    def at_y(step):
        return lax.rem(y + step + tall, tall)

    other_core = {"seq": seq_index(tall, z, y, 1 - core)}
    z_partners = {k: {"seq": seq_index(tall, at_z(k), y, core)} for k in range(1, DEPTH)}
    y_partners = {j: {"seq": seq_index(tall, z, at_y(j), core)} for j in range(1, tall)}
    x_partners = {i: {"mp": lax.rem(part + i, wide)} for i in range(1, wide)}
    greet(
        [other_core, *z_partners.values(), *y_partners.values(), *x_partners.values()]
    )

    def slot(piece, zz, yy, cc):
        place, start, width = pieces[piece]
        return outs[place].at[zz, yy, cc, :, pl.ds(start, width)]

    def own(piece):
        place, start, width = pieces[piece]
        return ins[place].at[:, pl.ds(start, width)]

    waits = []

    def begin(copy):
        copy.start()
        waits.append(copy)

    def send_y(piece, k):
        source = own(piece) if k == 0 else slot(piece, at_z(-k), y, core)
        for j in range(1, tall):
            begin(
                remote(
                    source,
                    slot(piece, at_z(-k), y, core),
                    y_send.at[piece, k, j],
                    y_recv.at[piece, k, j],
                    y_partners[j],
                )
            )

    def send_core(piece, k, j):
        target = slot(piece, at_z(-k), at_y(-j), core)
        source = own(piece) if k == 0 and j == 0 else target
        begin(
            remote(
                source, target, c_send.at[piece, k, j], c_recv.at[piece, k, j], other_core
            )
        )

    for piece in range(len(pieces)):
        for k in range(1, DEPTH):
            begin(
                remote(
                    own(piece),
                    slot(piece, z, y, core),
                    z_send.at[piece, k],
                    z_recv.at[piece, k],
                    z_partners[k],
                )
            )
        send_y(piece, 0)
        if piece == 0:
            for index in range(halves):
                for i in range(1, wide):
                    begin(
                        remote(
                            rows_in[index],
                            rows_out[index].at[part],
                            x_send.at[index, i],
                            x_recv.at[index, i],
                            x_partners[i],
                        )
                    )
    locals_ = []
    for place in range(arrays):
        copy = pltpu.make_async_copy(
            ins[place], outs[place].at[z, y, core], own_sem.at[place]
        )
        copy.start()
        locals_.append(copy)
    for index in range(halves):
        copy = pltpu.make_async_copy(
            rows_in[index], rows_out[index].at[part], own_sem.at[arrays + index]
        )
        copy.start()
        locals_.append(copy)
    for piece in range(len(pieces)):
        send_core(piece, 0, 0)

    def from_z(piece):
        for k in range(1, DEPTH):
            landed = slot(piece, at_z(-k), y, core)
            remote(
                landed, landed, z_send.at[piece, k], z_recv.at[piece, k], z_partners[k]
            ).wait_recv()
            send_y(piece, k)
            send_core(piece, k, 0)

    def from_y(piece):
        for k in range(DEPTH):
            for j in range(1, tall):
                landed = slot(piece, at_z(-k), at_y(-j), core)
                remote(
                    landed,
                    landed,
                    y_send.at[piece, k, j],
                    y_recv.at[piece, k, j],
                    y_partners[j],
                ).wait_recv()
                send_core(piece, k, j)

    for piece in range(len(pieces) + 1):
        if piece < len(pieces):
            from_z(piece)
        if piece > 0:
            from_y(piece - 1)
    for piece in range(len(pieces)):
        for k in range(DEPTH):
            for j in range(tall):
                landed = slot(piece, at_z(-k), at_y(-j), 1 - core)
                remote(
                    landed,
                    landed,
                    c_send.at[piece, k, j],
                    c_recv.at[piece, k, j],
                    other_core,
                ).wait_recv()
    for index in range(halves):
        for i in range(1, wide):
            landed = rows_out[index].at[lax.rem(part - i + wide, wide)]
            remote(
                landed, landed, x_send.at[index, i], x_recv.at[index, i], x_partners[i]
            ).wait_recv()
    for copy in waits:
        copy.wait_send()
    for copy in locals_:
        copy.wait()


def gather_all(shards, row_parts, seq, wide):
    tall = seq // (DEPTH * CORES)
    pieces = pieces_of([shard.shape[1] for shard in shards], 1536)
    count = len(pieces)
    moved = sum(shard.size * shard.dtype.itemsize for shard in shards) * seq
    dma = pltpu.SemaphoreType.DMA
    halves = len(row_parts)
    results = pl.pallas_call(
        functools.partial(gather_kernel, pieces, len(shards), halves, tall, wide),
        out_shape=[
            jax.ShapeDtypeStruct((DEPTH, tall, CORES) + shard.shape, shard.dtype)
            for shard in shards
        ]
        + [jax.ShapeDtypeStruct((wide,) + part.shape, part.dtype) for part in row_parts],
        in_specs=[pl.BlockSpec(memory_space=pl.ANY)] * (len(shards) + halves),
        out_specs=[pl.BlockSpec(memory_space=pl.ANY)] * (len(shards) + halves),
        scratch_shapes=[
            dma((len(shards) + halves,)),
            dma((count, DEPTH)),
            dma((count, DEPTH)),
            dma((count, DEPTH, tall)),
            dma((count, DEPTH, tall)),
            dma((count, DEPTH, tall)),
            dma((count, DEPTH, tall)),
            dma((halves, wide)),
            dma((halves, wide)),
        ],
        compiler_params=pltpu.CompilerParams(collective_id=0, has_side_effects=True),
        cost_estimate=pl.CostEstimate(flops=0, bytes_accessed=16 * moved, transcendentals=0),
        name="gather_weights",
    )(*shards, *row_parts)
    return results[: len(shards)], results[len(shards) :]


def scatter_kernel(pieces, arrays, tall, *refs):
    ins = refs[:arrays]
    outs = refs[arrays : 2 * arrays]
    rest = refs[2 * arrays :]
    from_core = rest[:arrays]
    from_y = rest[arrays : 2 * arrays]
    summed = rest[2 * arrays : 3 * arrays]
    from_z = rest[3 * arrays : 4 * arrays]
    c_send, c_recv, y_send, y_recv, z_send, z_recv = rest[4 * arrays :]
    z, y, core = seq_place(tall)

    def at_z(step):
        return lax.rem(z + step + DEPTH, DEPTH)

    def at_y(step):
        return lax.rem(y + step + tall, tall)

    other_core = {"seq": seq_index(tall, z, y, 1 - core)}
    z_partners = {k: {"seq": seq_index(tall, at_z(k), y, core)} for k in range(1, DEPTH)}
    y_partners = {j: {"seq": seq_index(tall, z, at_y(j), core)} for j in range(1, tall)}
    greet([other_core, *z_partners.values(), *y_partners.values()])

    def core_copy(piece):
        place, start, width = pieces[piece]
        cols = pl.ds(start, width)
        return remote(
            ins[place].at[:, :, 1 - core, :, cols],
            from_core[place].at[:, :, :, cols],
            c_send.at[piece],
            c_recv.at[piece],
            other_core,
        )

    def y_copy(piece, j):
        place, start, width = pieces[piece]
        cols = pl.ds(start, width)
        return remote(
            from_core[place].at[:, at_y(j), :, cols],
            from_y[place].at[j - 1, :, :, cols],
            y_send.at[piece, j],
            y_recv.at[piece, j],
            y_partners[j],
        )

    def z_copy(piece, k):
        place, start, width = pieces[piece]
        cols = pl.ds(start, width)
        return remote(
            summed[place].at[at_z(k), :, cols],
            from_z[place].at[k - 1, :, cols],
            z_send.at[piece, k],
            z_recv.at[piece, k],
            z_partners[k],
        )

    def after_core(piece):
        place, start, width = pieces[piece]
        cols = pl.ds(start, width)
        core_copy(piece).wait_recv()

        def add(block, carry):
            zz = block // tall
            yy = lax.rem(block, tall)
            total = ins[place][zz, yy, core, :, cols].astype(jnp.float32) + from_core[place][
                zz, yy, :, cols
            ].astype(jnp.float32)
            from_core[place][zz, yy, :, cols] = total.astype(from_core[place].dtype)
            return carry

        lax.fori_loop(0, DEPTH * tall, add, 0)
        for j in range(1, tall):
            y_copy(piece, j).start()

    def after_y(piece):
        place, start, width = pieces[piece]
        cols = pl.ds(start, width)
        for j in range(1, tall):
            y_copy(piece, j).wait_recv()

        def add(zz, carry):
            total = from_core[place][zz, y, :, cols].astype(jnp.float32)
            for j in range(1, tall):
                total = total + from_y[place][j - 1, zz, :, cols].astype(jnp.float32)
            summed[place][zz, :, cols] = total.astype(summed[place].dtype)
            return carry

        lax.fori_loop(0, DEPTH, add, 0)
        for k in range(1, DEPTH):
            z_copy(piece, k).start()

    def after_z(piece):
        place, start, width = pieces[piece]
        cols = pl.ds(start, width)
        for k in range(1, DEPTH):
            z_copy(piece, k).wait_recv()
        total = summed[place][z, :, cols].astype(jnp.float32)
        for k in range(1, DEPTH):
            total = total + from_z[place][k - 1, :, cols].astype(jnp.float32)
        outs[place][:, cols] = total

    count = len(pieces)
    for piece in range(count):
        core_copy(piece).start()
    for piece in range(count + 4):
        if piece < count:
            after_core(piece)
        if 2 <= piece < count + 2:
            after_y(piece - 2)
        if 4 <= piece:
            after_z(piece - 4)
    for piece in range(count):
        core_copy(piece).wait_send()
        for j in range(1, tall):
            y_copy(piece, j).wait_send()
        for k in range(1, DEPTH):
            z_copy(piece, k).wait_send()


def scatter_all(terms, seq):
    tall = seq // (DEPTH * CORES)
    terms = [
        term.reshape((DEPTH, tall, CORES, term.shape[0] // seq, term.shape[1])) for term in terms
    ]
    blocks = [term.shape[3:] for term in terms]
    kinds = [term.dtype for term in terms]
    pieces = pieces_of([block[1] for block in blocks], 768)
    count = len(pieces)
    pairs = list(zip(blocks, kinds))
    dma = pltpu.SemaphoreType.DMA
    return pl.pallas_call(
        functools.partial(scatter_kernel, pieces, len(terms), tall),
        out_shape=[jax.ShapeDtypeStruct(block, jnp.float32) for block in blocks],
        in_specs=[pl.BlockSpec(memory_space=pltpu.VMEM)] * len(terms),
        out_specs=[pl.BlockSpec(memory_space=pltpu.VMEM)] * len(terms),
        scratch_shapes=[pltpu.VMEM((DEPTH, tall) + block, kind) for block, kind in pairs]
        + [pltpu.VMEM((max(1, tall - 1), DEPTH) + block, kind) for block, kind in pairs]
        + [pltpu.VMEM((DEPTH,) + block, kind) for block, kind in pairs]
        + [pltpu.VMEM((DEPTH - 1,) + block, kind) for block, kind in pairs]
        + [
            dma((count,)),
            dma((count,)),
            dma((count, tall)),
            dma((count, tall)),
            dma((count, DEPTH)),
            dma((count, DEPTH)),
        ],
        compiler_params=pltpu.CompilerParams(
            collective_id=1, has_side_effects=True, vmem_limit_bytes=VMEM_BYTES
        ),
        name="scatter_grads",
    )(*terms)


def mp_gather(value, axis):
    if lax.axis_size("mp") != 2:
        return lax.all_gather(value, "mp", axis=axis, tiled=True)
    other = lax.ppermute(value, "mp", [(0, 1), (1, 0)])
    first = lax.axis_index("mp") == 0
    return jnp.concatenate(
        [jnp.where(first, value, other), jnp.where(first, other, value)], axis=axis
    )


def mp_sum(value):
    if lax.axis_size("mp") != 2:
        return lax.psum(value, "mp")
    other = lax.ppermute(value.astype(jnp.bfloat16), "mp", [(0, 1), (1, 0)])
    return value + other.astype(jnp.float32)


def mp_sum_own(value, rows):
    if lax.axis_size("mp") != 2:
        return lax.psum_scatter(value, "mp", scatter_dimension=0, tiled=True)
    place = lax.axis_index("mp")
    sent = lax.dynamic_slice_in_dim(value, (1 - place) * rows, rows, 0).astype(jnp.bfloat16)
    other = lax.ppermute(sent, "mp", [(0, 1), (1, 0)])
    return lax.dynamic_slice_in_dim(value, place * rows, rows, 0) + other.astype(jnp.float32)


def on_device(tokens, positions, counts, cotangent, gains, in_w, out_w, gate_up, down_w, conv_w):
    rows, width = tokens.shape
    group = positions.shape[0]
    count = counts[0]
    seq = lax.axis_size("seq")
    wide = lax.axis_size("mp")
    mp_place = lax.axis_index("mp")
    depth = in_w.shape[0]
    chans = in_w.shape[2]
    units = gate_up.shape[2]
    gain_cols = width // seq
    tap_cols = chans // seq

    small = jnp.zeros((16, LANES), jnp.bfloat16)
    small = small.at[:2, :gain_cols].set(mp_gather(gains, 1))
    small = small.at[2:5, :tap_cols].set(conv_w)
    gathered, whole_rows = gather_all(
        [
            small,
            in_w.reshape(depth, 3 * chans),
            out_w.T,
            gate_up.reshape(depth, 2 * units),
            down_w.T,
        ],
        [tokens, cotangent],
        seq,
        wide,
    )
    small_all = gathered[0].reshape(seq, 16, LANES).astype(jnp.float32)
    in_flat = gathered[1].reshape(width, 3 * chans)
    out_turned = gathered[2].reshape(width, chans)
    gu_flat = gathered[3].reshape(width, 2 * units)
    down_turned = gathered[4].reshape(width, units)
    gain_all = small_all[:, :2, :gain_cols].transpose(1, 0, 2).reshape(2, width)
    conv_taps = small_all[:, 2:5, :tap_cols].transpose(1, 0, 2).reshape(3, chans)
    inputs = whole_rows[0].reshape(group, width).astype(jnp.float32)
    valid = (jnp.arange(group, dtype=jnp.int32) < count)[:, None]
    grad_all = whole_rows[1].reshape(group, width)
    grad_all = jnp.where(valid, grad_all, jnp.zeros_like(grad_all))

    def own(value):
        return lax.dynamic_slice_in_dim(value, mp_place * rows, rows, 0)

    scale_one = norm_scale(inputs)
    mixer_all = (inputs * scale_one * gain_all[0]).astype(jnp.bfloat16)
    proj = jnp.dot(mixer_all, in_flat, preferred_element_type=jnp.float32)
    bgate = proj[:, :chans]
    cgate = proj[:, chans : 2 * chans]
    xin = proj[:, 2 * chans :]
    gated = (bgate * xin).astype(jnp.bfloat16)
    tail = lax.dynamic_slice_in_dim(gated, count - 2, 2, 0)
    before = from_behind(tail, "seq", 1)
    extended = jnp.concatenate([before, gated], axis=0).astype(jnp.float32)
    one_back = extended[1 : group + 1]
    two_back = extended[:group]
    keep_one = (positions >= 1).astype(jnp.float32)[:, None]
    keep_two = (positions >= 2).astype(jnp.float32)[:, None]
    current = gated.astype(jnp.float32)
    conv = (
        conv_taps[2] * current
        + keep_one * conv_taps[1] * one_back
        + keep_two * conv_taps[0] * two_back
    )
    mixed_in = (cgate * conv).astype(jnp.bfloat16)
    resid = inputs + mp_sum(contract_cols(mixed_in, out_turned))
    scale_two = norm_scale(resid)
    ff_all = (resid * scale_two * gain_all[1]).astype(jnp.bfloat16)
    both = jnp.dot(ff_all, gu_flat, preferred_element_type=jnp.float32)
    gate = both[:, :units]
    upper = both[:, units:]
    sigma = jax.nn.sigmoid(gate)
    active = gate * sigma
    hidden = (active * upper).astype(jnp.bfloat16)
    final = own(resid) + mp_sum_own(contract_cols(hidden, down_turned), rows)
    mixed = jnp.where(own(valid), final, jnp.zeros_like(final)).astype(jnp.bfloat16)

    grad_hidden = jnp.dot(grad_all, down_turned, preferred_element_type=jnp.float32)
    slope = sigma * (1.0 + gate * (1.0 - sigma))
    grad_both = jnp.concatenate([grad_hidden * upper * slope, grad_hidden * active], axis=1).astype(
        jnp.bfloat16
    )
    term_down = contract_rows(grad_all, hidden).astype(jnp.bfloat16)
    term_gu = contract_rows(ff_all, grad_both).astype(jnp.bfloat16)
    back_two = mp_sum(contract_cols(grad_both, gu_flat))
    grad_resid = grad_all.astype(jnp.float32) + norm_back(resid, scale_two, gain_all[1], back_two)
    gain_two = jnp.sum(own(back_two * resid * scale_two), axis=0)
    grad_o_all = grad_resid.astype(jnp.bfloat16)
    term_out = contract_rows(grad_o_all, mixed_in).astype(jnp.bfloat16)
    grad_mix = jnp.dot(grad_o_all, out_turned, preferred_element_type=jnp.float32)
    grad_cgate = grad_mix * conv
    grad_conv = grad_mix * cgate
    lead_one = keep_one * grad_conv
    lead_two = keep_two * grad_conv
    head = jnp.stack(
        [conv_taps[0] * lead_two[0], conv_taps[1] * lead_one[0] + conv_taps[0] * lead_two[1]]
    )
    after = from_behind(head, "seq", -1)
    zero_one = jnp.zeros((1, chans), jnp.float32)
    zero_two = jnp.zeros((2, chans), jnp.float32)
    row_ids = jnp.arange(group, dtype=jnp.int32)[:, None]
    border = jnp.where(row_ids == count - 2, after[:1], jnp.where(row_ids == count - 1, after[1:], 0.0))
    grad_gated = (
        conv_taps[2] * grad_conv
        + conv_taps[1] * jnp.concatenate([lead_one[1:], zero_one], axis=0)
        + conv_taps[0] * jnp.concatenate([lead_two[2:], zero_two], axis=0)
        + border
    )
    term_conv = jnp.stack(
        [
            jnp.sum(lead_two * two_back, axis=0),
            jnp.sum(lead_one * one_back, axis=0),
            jnp.sum(grad_conv * current, axis=0),
        ]
    )
    grad_proj = jnp.concatenate([grad_gated * xin, grad_cgate, grad_gated * bgate], axis=1).astype(
        jnp.bfloat16
    )
    term_in = contract_rows(mixer_all, grad_proj).astype(jnp.bfloat16)
    back_one = mp_sum_own(contract_cols(grad_proj, in_flat), rows)
    own_inputs = own(inputs)
    own_scale = own(scale_one)
    grad_input = (
        own(grad_resid) + norm_back(own_inputs, own_scale, gain_all[0], back_one)
    ).astype(jnp.bfloat16)
    gain_one = jnp.sum(back_one * own_inputs * own_scale, axis=0)
    gain_terms = jnp.stack([gain_one, gain_two]).reshape(2, seq, gain_cols).transpose(1, 0, 2)
    tap_terms = term_conv.reshape(3, seq, tap_cols).transpose(1, 0, 2)
    small_terms = jnp.zeros((seq, 8, LANES), jnp.float32)
    small_terms = small_terms.at[:, :2, :gain_cols].set(gain_terms)
    small_terms = small_terms.at[:, 2:5, :tap_cols].set(tap_terms)
    sum_gu, sum_down, sum_out, sum_in, sum_small = scatter_all(
        [term_gu, term_down, term_out, term_in, small_terms.reshape(seq * 8, LANES)], seq
    )
    grad_gains = lax.psum_scatter(
        sum_small[:2, :gain_cols], "mp", scatter_dimension=1, tiled=True
    ) if wide != 2 else gain_share(sum_small[:2, :gain_cols], mp_place)
    return (
        mixed,
        grad_input,
        grad_gains,
        sum_in.reshape(depth, 3, chans),
        sum_out.T,
        sum_gu.reshape(depth, 2, units),
        sum_down.T,
        sum_small[2:5, :tap_cols],
    )


def gain_share(sums, place):
    cols = sums.shape[1] // 2
    total = sums + lax.ppermute(sums, "mp", [(0, 1), (1, 0)])
    return lax.dynamic_slice_in_dim(total, place * cols, cols, 1)


def solution(mesh):
    placed = (
        P(("seq", "mp"), None),
        P("seq"),
        P("seq"),
        P(("seq", "mp"), None),
        P(None, ("seq", "mp")),
        P("seq", None, "mp"),
        P("mp", "seq"),
        P("seq", None, "mp"),
        P("mp", "seq"),
        P(None, ("mp", "seq")),
    )
    return jax.shard_map(
        on_device,
        mesh=mesh,
        in_specs=placed,
        out_specs=(
            P(("seq", "mp"), None),
            P(("seq", "mp"), None),
            P(None, ("seq", "mp")),
            P("seq", None, "mp"),
            P("mp", "seq"),
            P("seq", None, "mp"),
            P("mp", "seq"),
            P(None, ("mp", "seq")),
        ),
        check_vma=False,
    )
```

time: 961 us -> 358 us (0.37)
  waiting for transfers between devices: 706 us -> 21.5 us
  Pallas kernels: 0 us -> 252 us
  blocking collectives: 124 us -> 0 us
  local copies, waits for them, and re-layouts: 45.7 us -> 19 us
  between operations: 15.6 us -> 1.8 us
  matrix products: 47.9 us -> 36 us
    unnamed x16 -> x0, waiting for transfers between devices: 406 us -> none
    pallas_call x0 -> x2, Pallas kernels: none -> 252 us  [the longest x1 128 us: scatter_all(): pl.pallas_call(functools.partial(scatter_kernel, pieces, len(terms), tall...]
    reduce_scatter x6 -> x0, waiting for transfers between devices: 190 us -> none  [the longest x1 76.8 us: on_device(): lax.psum_scatter(term_down.astype(jnp.bfloat16), 'seq', scatter_dimension...]
    all_gather x6 -> x0, blocking collectives: 124 us -> none  [the longest x1 69.6 us: on_device(): lax.all_gather(gains, ('seq', 'mp'), axis=1, tiled=True).astype(jnp.float32)]
    all_gather x4 -> x0, waiting for transfers between devices: 108 us -> none  [the longest x1 71.3 us: on_device(): lax.all_gather(gate_up, 'seq', axis=0, tiled=True)]
    convert_element_type x5 -> x2, local copies, waits for them, and re-layouts: 22.2 us -> 0.08 us  [mp_sum_own(): lax.dynamic_slice_in_dim(value, (1 - place) * rows, rows, 0)]
    ppermute x0 -> x6, waiting for transfers between devices: none -> 21.2 us  [the longest x2 15.2 us: mp_sum(): other = lax.ppermute(value.astype(jnp.bfloat16), 'mp', [(0, 1), (1, 0)])]
    unnamed x51 -> x53, local copies, waits for them, and re-layouts: 18.2 us -> 5.66 us
  transfers between devices with their start and end apart: 15 -> 8, of which waited for: 13 -> 4; matrix products, arithmetic and copies ran while one was open for 9% -> 10% of each run, Pallas kernels for 0% -> 0%
where the time goes in v1:
time: 358 us; the launch traced here: 357 us
  Pallas kernels  252 us (70%)
  matrix products  36 us (10%)
  waiting for transfers between devices  21.5 us (6%)
  local copies, waits for them, and re-layouts  19 us (5%)
  other arithmetic  16 us (4%)
  starting transfers between devices  10.6 us (3%)
    pallas_call x1, Pallas kernels, scatter_all(): pl.pallas_call(functools.partial(scatter_kernel, pieces, len(terms), tall...  128 us
    pallas_call x1, Pallas kernels, gather_all(): pl.pallas_call(functools.partial(gather_kernel, pieces, len(shards), halv...  124 us
    ppermute x2, waiting for transfers between devices, mp_sum(): other = lax.ppermute(value.astype(jnp.bfloat16), 'mp', [(0, 1), (1, 0)])  15.2 us
    dot_general x4, matrix products, contract_rows(): lax.dot_general(left, right, (((0,), (0,)), ((), ())), preferred_element_...  13.2 us
    dot_general x4, matrix products, contract_cols(): lax.dot_general(left, right, (((1,), (1,)), ((), ())), preferred_element_...  11.1 us
  transfers between devices with their start and end apart: 8, of which 4 were waited for; matrix products, arithmetic and copies ran while one was open for 10% of the time, Pallas kernels for 0%

profile of v1, /device:TPU:0, one launch (start us, length us, event | category | flops | bytes accessed | tf_op | source)
XLA Modules:
  0.0 357.1 jit_solution(11368216741746663882)
XLA Ops:
  0.6 3.0 collective-permute-start
  3.6 1.9 copy.24
  5.6 1.6 copy.23
  9.3 1.5 scatter.15.refs_0_
  11.4 124.3 %gather_weights.1 = (bf16[4,2,2,16,128]{4,3,2,1,0:T(8,128)(2,1)}, bf16[4,2,2,64,1536]{4,3,2,1,0:T(8,128)(2,1)}, bf16[4,2,2,64,512]{4,3,2,1,0:T(8,128)(2,1)}, bf1...) custom-call(bf16[16,128]{1,0:T(8,128)(2,1)} %copy-done.19, ...), custom_call_target="tpu_custom_call" | custom-call | bytes 294649856 | tf_op jit(solution)/shard_map/gather_weights/pallas_call | solution.py:241
  136.8 1.2 multiply_reduce_fusion.2
  138.0 1.2 multiply_convert_fusion.5
  139.2 2.9 fusion.33
  142.2 2.8 collective-permute-start.1
  146.0 1.7 fusion.30
  149.5 1.1 broadcast_select_fusion
  150.6 11.7 %collective-permute-done.2 = bf16[256,1024]{1,0:T(8,128)(2,1)} collective-permute-done((bf16[256,1024]{1,0:T(8,128)(2,1)}, bf16[256,1024]{1,0:T(8,128)(2,1)}, u32[]{:S(2)}, u32[]{:S(2)}) %collective-permute-start.2) | collective-permute-done | bytes 524320 | tf_op jit(solution)/shard_map/ppermute | solution.py:434
  162.3 1.5 multiply_reduce_fusion.1
  163.8 5.4 %fusion.27 = f32[256,4608]{1,0:T(8,128)S(1)} fusion(bf16[1024,4608]{1,0:T(8,128)(2,1)} %bitcast.101, f32[256,1024]{1,0:T(8,128)S(1)} %get-tuple-element.115, f32[1024]{0:T(1024)S(1)} %mul.341, f32[256]{0:T(256)S(1)} %get-tuple-element.137), kind=kOutput, calls=%fused_computation.105 | convolution fusion | flops 2416705536 | bytes 15209472 | tf_op jit(solution)/shard_map/dot_general | solution.py:514
  169.3 1.9 multiply_convert_fusion.1
  171.3 2.6 fusion.31
  174.2 3.7 %fusion.34 = f32[256,1024]{1,0:T(8,128)S(1)} fusion(bf16[256,2304]{1,0:T(8,128)(2,1)S(1)} %get-tuple-element.118, bf16[1024,2304]{1,0:T(8,128)(2,1)} %bitcast.105), kind=kOutput, calls=%fused_computation.112 | convolution fusion | flops 1207959552 | bytes 6946816 | tf_op jit(solution)/shard_map/dot_general | solution.py:25
  178.0 1.8 collective-permute-start.3
  179.8 5.4 %convolution_convert_fusion = bf16[1024,4608]{1,0:T(8,128)(2,1)} fusion(bf16[256,2304]{1,0:T(8,128)(2,1)S(1)} %get-tuple-element.117, bf16[256,2304]{1,0:T(8,128)(2,1)S(1)} %get-tuple-element.116, f32[256,1024]{1,0:T(8,128)S(1)} %get-tuple-element.115, f32[1024]{0:T(1024)S(1)} %mul.341, f32[256]{0:T(256)S(1)} %get-tuple-element.137), kind=kOutput, calls=%fused_computation | convolution fusion | flops 2426142720 | bytes 12850176 | tf_op jit(solution)/shard_map/dot_general | solution.py:19
  185.2 3.6 %collective-permute-done.4 = bf16[256,1024]{1,0:T(8,128)(2,1)S(1)} collective-permute-done((bf16[256,1024]{1,0:T(8,128)(2,1)S(1)}, bf16[256,1024]{1,0:T(8,128)(2,1)S(1)}, u32[]{:S(2)}, u32[]{:S(2)}) %collective-permute-start.4) | collective-permute-done | bytes 524320 | tf_op jit(solution)/shard_map/ppermute | solution.py:434
  190.5 1.5 multiply_reduce_fusion.4
  192.0 1.5 collective-permute-start.5
  193.5 3.7 %convolution_convert_fusion.1 = bf16[1024,2304]{1,0:T(8,128)(2,1)} fusion(bf16[256,1024]{1,0:T(8,128)(2,1)S(1)} %get-tuple-element.111, bf16[256,2304]{1,0:T(8,128)(2,1)S(1)} %get-tuple-element.118), kind=kOutput, calls=%fused_computation.1 | convolution fusion | flops 1210318848 | bytes 6422528 | tf_op jit(solution)/shard_map/dot_general | solution.py:19
  197.2 1.4 convolution_convert_fusion.3
  201.6 2.5 multiply_convert_fusion.9
  204.2 1.1 multiply_convert_fusion.7
  205.3 3.0 fusion.9
  208.8 2.7 convolution_convert_fusion.2
  211.5 6.0 %collective-permute-done.6 = bf16[128,1024]{1,0:T(8,128)(2,1)S(1)} collective-permute-done((bf16[128,1024]{1,0:T(8,128)(2,1)S(1)}, bf16[128,1024]{1,0:T(8,128)(2,1)S(1)}, u32[]{:S(2)}, u32[]{:S(2)}) %collective-permute-start.6) | collective-permute-done | bytes 262176 | tf_op jit(solution)/shard_map/ppermute | solution.py:443
  219.2 127.9 %scatter_grads.1 = (f32[64,4608]{1,0:T(8,128)}, f32[64,2304]{1,0:T(8,128)}, f32[64,512]{1,0:T(8,128)}, f32[64,1536]{1,0:T(8,128)}, f32[8,128]{1,0:T(8,128)}) custom-call(bf16[4,2,2,64,4608]{4,3,2,1,0:T(8,128)(2,1)} %bitcast.73, bf16[4,2,2,64,2304]{4,3,2,1,0:T(8,128)(2,1)} %bitcast.74, bf16[4,2,2,64,512]{4,3,2,1,0:T(8,128)(2,1)} %bitcast.77, ...), custom_call_target="tpu_custom_call" | custom-call | tf_op jit(solution)/shard_map/scatter_grads/pallas_call | solution.py:397
  347.8 1.2 slice.201
  350.4 3.1 reshape.319
  (118 shorter events, 18.7 us)
Async XLA Ops:
  0.6 7.9 %collective-permute-start = (bf16[2,32]{1,0:T(2,128)(2,1)}, bf16[2,32]{1,0:T(2,128)(2,1)S(1)}, u32[]{:S(2)}, u32[]{:S(2)}) collective-permute-start(bf16[2,32]{1,0:T(2,128)(2,1)} %param.22), channel_id=1, source_target_pairs={{0,1},{1,0},{2,3},{3,2},{4,5},{5,4},{6,7},{7,6},{8,9},{9,8},{10,11... | collective-permute-start | bytes 392 | tf_op jit(solution)/shard_map/ppermute | solution.py:424
  142.1 3.9 %copy-start.5 = (bf16[4,2,2,64,512]{4,3,2,1,0:T(8,128)(2,1)S(1)}, bf16[4,2,2,64,512]{4,3,2,1,0:T(8,128)(2,1)}, u32[]{:S(2)}) copy-start(bf16[4,2,2,64,512]{4,3,2,1,0:T(8,128)(2,1)} %get-tuple-element.71) | copy-start | bytes 3145732
  142.2 3.4 collective-permute-start.1
  145.7 2.0 copy-start.1
  145.7 2.6 copy-start
  146.0 1.7 copy-start.7
  147.7 14.5 %copy-start.4 = (f32[256,1024]{1,0:T(8,128)S(1)}, f32[256,1024]{1,0:T(8,128)}, u32[]{:S(2)}) copy-start(f32[256,1024]{1,0:T(8,128)} %get-tuple-element.143) | copy-start | bytes 3145732
  147.7 14.5 %collective-permute-start.2 = (bf16[256,1024]{1,0:T(8,128)(2,1)}, bf16[256,1024]{1,0:T(8,128)(2,1)}, u32[]{:S(2)}, u32[]{:S(2)}) collective-permute-start(bf16[256,1024]{1,0:T(8,128)(2,1)} %get-tuple-element.142), channel_id=1, source_target_pairs={{0,1},{1,0},{2,3},{3,2},{4,5},{5,4},{6,7},{7,6},{8,9},{9,8},{10,11... | collective-permute-start | bytes 1572872 | tf_op jit(solution)/shard_map/ppermute | solution.py:434
  162.3 7.0 %slice-start.3 = ((s8[4718592]{0:T(1024)(128)(4,1)}), s8[4194304]{0:T(1024)(128)(4,1)S(1)}, s32[]{:S(2)}) async-start(s8[4718592]{0:T(1024)(128)(4,1)} %bitcast.106), calls=%async_computation.3 | async-start | bytes 8388608
  163.8 5.5 %slice-start.4 = ((s8[4718592]{0:T(1024)(128)(4,1)}), s8[524288]{0:T(1024)(128)(4,1)S(1)}, s32[]{:S(2)}) async-start(s8[4718592]{0:T(1024)(128)(4,1)} %bitcast.106), calls=%async_computation.4 | async-start | bytes 1048576
  163.8 7.4 %slice-start = ((s8[9437184]{0:T(1024)(128)(4,1)}), s8[4194304]{0:T(1024)(128)(4,1)S(1)}, s32[]{:S(2)}) async-start(s8[9437184]{0:T(1024)(128)(4,1)} %bitcast.102), calls=%async_computation | async-start | bytes 8388608
  163.8 7.4 %slice-start.1 = ((s8[9437184]{0:T(1024)(128)(4,1)}), s8[4194304]{0:T(1024)(128)(4,1)S(1)}, s32[]{:S(2)}) async-start(s8[9437184]{0:T(1024)(128)(4,1)} %bitcast.102), calls=%async_computation.1 | async-start | bytes 8388608
  169.3 1.9 slice-start.2
  173.9 14.9 %collective-permute-start.4 = (bf16[256,1024]{1,0:T(8,128)(2,1)S(1)}, bf16[256,1024]{1,0:T(8,128)(2,1)S(1)}, u32[]{:S(2)}, u32[]{:S(2)}) collective-permute-start(bf16[256,1024]{1,0:T(8,128)(2,1)S(1)} %get-tuple-element.144), channel_id=1, source_target_pairs={{0,1},{1,0},{2,3},{3,2},{4,5},{5,4},{6,7},{7,6},{8,9},{9,8},{10,11... | collective-permute-start | bytes 1572872 | tf_op jit(solution)/shard_map/ppermute | solution.py:434
  178.0 20.7 %collective-permute-start.3 = (bf16[128,1024]{1,0:T(8,128)(2,1)S(1)}, bf16[128,1024]{1,0:T(8,128)(2,1)S(1)}, u32[]{:S(2)}, u32[]{:S(2)}) collective-permute-start(bf16[128,1024]{1,0:T(8,128)(2,1)S(1)} %dynamic-slice_convert_fusion.1), channel_id=1, source_target_pairs={{0,1},{1,0},{2,3},{3,2},{4,5},{5,4},{6,7},{7,6},{8,9},{9,8},{10,11... | collective-permute-start | bytes 786440 | tf_op jit(solution)/shard_map/ppermute | solution.py:443
  185.2 3.9 %copy-start.9 = (bf16[2,128,1024]{2,1,0:T(8,128)(2,1)S(1)}, bf16[2,128,1024]{2,1,0:T(8,128)(2,1)}, u32[]{:S(2)}) copy-start(bf16[2,128,1024]{2,1,0:T(8,128)(2,1)} %get-tuple-element.74) | copy-start | bytes 1572868
  189.1 1.1 copy-start.2
  189.1 1.4 copy-start.6
  192.0 9.5 %collective-permute-start.5 = (f32[2,512]{1,0:T(2,128)S(1)}, f32[2,512]{1,0:T(2,128)S(1)}, u32[]{:S(2)}, u32[]{:S(2)}) collective-permute-start(f32[2,512]{1,0:T(2,128)S(1)} %pad_maximum_fusion.6), channel_id=1, source_target_pairs={{2,0},{4,2},{6,4},{8,6},{10,8},{12,10},{14,12},{16,14},{18,16},{20... | collective-permute-start | bytes 12296 | tf_op jit(solution)/shard_map/ppermute | solution.py:43
  193.5 3.7 %copy-start.8 = (bf16[256,512]{1,0:T(8,128)(2,1)S(1)}, bf16[256,512]{1,0:T(8,128)(2,1)}, u32[]{:S(2)}) copy-start(bf16[256,512]{1,0:T(8,128)(2,1)} %copy-done.7) | copy-start | bytes 786436
  201.5 3.7 %copy-start.15 = (bf16[256,512]{1,0:T(8,128)(2,1)S(1)}, bf16[256,512]{1,0:T(8,128)(2,1)}, u32[]{:S(2)}) copy-start(bf16[256,512]{1,0:T(8,128)(2,1)} %get-tuple-element.119) | copy-start | bytes 786436
  205.3 3.5 copy-start.16
  205.3 3.5 copy-start.17
  208.4 9.1 %copy-start.10 = (f32[256,1024]{1,0:T(8,128)}, f32[256,1024]{1,0:T(8,128)S(1)}, u32[]{:S(2)}) copy-start(f32[256,1024]{1,0:T(8,128)S(1)} %fusion.9) | copy-start | bytes 3145732
  208.4 9.1 %collective-permute-start.6 = (bf16[128,1024]{1,0:T(8,128)(2,1)S(1)}, bf16[128,1024]{1,0:T(8,128)(2,1)S(1)}, u32[]{:S(2)}, u32[]{:S(2)}) collective-permute-start(bf16[128,1024]{1,0:T(8,128)(2,1)S(1)} %dynamic-slice_convert_fusion), channel_id=1, source_target_pairs={{0,1},{1,0},{2,3},{3,2},{4,5},{5,4},{6,7},{7,6},{8,9},{9,8},{10,11... | collective-permute-start | bytes 786440 | tf_op jit(solution)/shard_map/ppermute | solution.py:443
  208.8 8.7 %copy-start.3 = (f32[256,1024]{1,0:T(8,128)S(1)}, f32[256,1024]{1,0:T(8,128)}, u32[]{:S(2)}) copy-start(f32[256,1024]{1,0:T(8,128)} %convert.29) | copy-start | bytes 3145732
  218.5 0.6 copy-start.14
  219.2 130.4 %copy-start.11 = (f32[256,1024]{1,0:T(8,128)S(1)}, f32[256,1024]{1,0:T(8,128)}, u32[]{:S(2)}) copy-start(f32[256,1024]{1,0:T(8,128)} %copy-done.10) | copy-start | bytes 3145732
  347.0 6.5 %copy-start.13 = (f32[64,1536]{1,0:T(8,128)S(1)}, f32[64,1536]{1,0:T(8,128)}, u32[]{:S(2)}) copy-start(f32[64,1536]{1,0:T(8,128)} %get-tuple-element.76) | copy-start | bytes 1179652
  349.0 5.3 %collective-permute-start.7 = (f32[2,64]{1,0:T(2,128)S(1)}, f32[2,64]{1,0:T(2,128)S(1)}, u32[]{:S(2)}, u32[]{:S(2)}) collective-permute-start(f32[2,64]{1,0:T(2,128)S(1)} %slice.200), channel_id=1, source_target_pairs={{0,1},{1,0},{2,3},{3,2},{4,5},{5,4},{6,7},{7,6},{8,9},{9,8},{10,11... | collective-permute-start | bytes 1544 | tf_op jit(solution)/shard_map/ppermute | solution.py:597
  349.5 6.1 %copy-start.18 = (f32[64,512]{1,0:T(8,128)S(1)}, f32[64,512]{1,0:T(8,128)}, u32[]{:S(2)}) copy-start(f32[64,512]{1,0:T(8,128)} %get-tuple-element.77) | copy-start | bytes 393220
  350.4 5.9 %copy-start.12 = (f32[64,2304]{1,0:T(8,128)S(1)}, f32[64,2304]{1,0:T(8,128)}, u32[]{:S(2)}) copy-start(f32[64,2304]{1,0:T(8,128)} %get-tuple-element.79) | copy-start | bytes 1769476
  (1 other events, 0.6 us)

commit v2 on v1

--- a/solution.py
+++ b/solution.py
@@ -418,6 +418,321 @@
     )(*terms)
 
 
+def mixer_back_kernel(pieces, ready, *refs):
+    (gu_hbm, down_hbm, sent_two, part_two, resid, grad_all, tokens, mixer, mixed_in, conv, cgate, xin,
+     bgate, current, one_back, two_back, masks, out_w, in_w, gain, taps) = refs[:21]
+    sum_gu, sum_down, sum_out, sum_in, grad_input, small = refs[21:27]
+    rest = refs[27:]
+    own_gu, own_down, term_out, term_in = rest[:4]
+    from_core = rest[4:8]
+    from_y = rest[8:12]
+    from_z = rest[12:16]
+    (recv_two, grad_resid, grad_o, grad_proj, part_one, send_one, recv_one, head, after, lead_one_ref,
+     lead_two_ref, gconv_ref, small_send, small_core, small_y, small_z, small_x) = rest[16:33]
+    (l_sem, c_send, c_recv, y_send, y_recv, z_send, z_recv, x_send, x_recv, h_sem, s_send, s_recv) = rest[33:]
+    outs = (sum_gu, sum_down, sum_out, sum_in)
+    terms = (gu_hbm, down_hbm, term_out, term_in)
+    tall = 2
+    total_seq = DEPTH * tall * CORES
+    group = resid.shape[0]
+    rows = grad_input.shape[0]
+    chans = conv.shape[1]
+    z, y, core = seq_place(tall)
+    here = lax.axis_index("seq")
+    part = lax.axis_index("mp")
+
+    def at_z(step):
+        return lax.rem(z + step + DEPTH, DEPTH)
+
+    other_core = {"seq": seq_index(tall, z, y, 1 - core)}
+    z_partners = {k: {"seq": seq_index(tall, at_z(k), y, core)} for k in range(1, DEPTH)}
+    y_partner = {"seq": seq_index(tall, z, 1 - y, core)}
+    x_partner = {"mp": 1 - part}
+    earlier = {"seq": lax.rem(here + total_seq - 1, total_seq)}
+    later = {"seq": lax.rem(here + 1, total_seq)}
+    greet([other_core, *z_partners.values(), y_partner, x_partner, earlier, later])
+
+    def core_copy(piece):
+        place, start, width = pieces[piece]
+        cols = pl.ds(start, width)
+        return remote(terms[place].at[:, :, 1 - core, :, cols], from_core[place].at[:, :, :, cols],
+                      c_send.at[piece], c_recv.at[piece], other_core)
+
+    def own_copy(piece):
+        place, start, width = pieces[piece]
+        cols = pl.ds(start, width)
+        return pltpu.make_async_copy(terms[place].at[:, :, core, :, cols],
+                                     (own_gu, own_down)[place].at[:, :, :, cols], l_sem.at[piece])
+
+    def y_copy(piece):
+        place, start, width = pieces[piece]
+        cols = pl.ds(start, width)
+        return remote(from_core[place].at[:, 1 - y, :, cols], from_y[place].at[:, :, cols],
+                      y_send.at[piece], y_recv.at[piece], y_partner)
+
+    def z_copy(piece, k):
+        place, start, width = pieces[piece]
+        cols = pl.ds(start, width)
+        return remote(from_y[place].at[at_z(k), :, cols], from_z[place].at[k - 1, :, cols],
+                      z_send.at[piece, k], z_recv.at[piece, k], z_partners[k])
+
+    def after_core(piece):
+        place, start, width = pieces[piece]
+        cols = pl.ds(start, width)
+        if piece < ready:
+            own_copy(piece).wait()
+        core_copy(piece).wait_recv()
+
+        def add(block, carry):
+            zz = block // tall
+            yy = lax.rem(block, tall)
+            if place < 2:
+                mine = (own_gu, own_down)[place][zz, yy, :, cols]
+            else:
+                mine = terms[place][zz, yy, core, :, cols]
+            total = mine.astype(jnp.float32) + from_core[place][zz, yy, :, cols].astype(jnp.float32)
+            from_core[place][zz, yy, :, cols] = total.astype(jnp.bfloat16)
+            return carry
+
+        lax.fori_loop(0, DEPTH * tall, add, 0)
+        y_copy(piece).start()
+
+    def after_y(piece):
+        place, start, width = pieces[piece]
+        cols = pl.ds(start, width)
+        y_copy(piece).wait_recv()
+
+        def add(zz, carry):
+            total = from_core[place][zz, y, :, cols].astype(jnp.float32) + from_y[place][
+                zz, :, cols
+            ].astype(jnp.float32)
+            from_y[place][zz, :, cols] = total.astype(jnp.bfloat16)
+            return carry
+
+        lax.fori_loop(0, DEPTH, add, 0)
+        for k in range(1, DEPTH):
+            z_copy(piece, k).start()
+
+    def after_z(piece):
+        place, start, width = pieces[piece]
+        cols = pl.ds(start, width)
+        for k in range(1, DEPTH):
+            z_copy(piece, k).wait_recv()
+        total = from_y[place][z, :, cols].astype(jnp.float32)
+        for k in range(1, DEPTH):
+            total = total + from_z[place][k - 1, :, cols].astype(jnp.float32)
+        outs[place][:, cols] = total
+
+    two_copy = remote(sent_two, recv_two, x_send.at[0], x_recv.at[0], x_partner)
+    one_copy = remote(send_one, recv_one, x_send.at[1], x_recv.at[1], x_partner)
+    head_copy = remote(head, after, h_sem.at[0], h_sem.at[1], earlier)
+
+    count = len(pieces)
+    two_copy.start()
+    for piece in range(ready):
+        core_copy(piece).start()
+        own_copy(piece).start()
+    for piece in range(ready):
+        after_core(piece)
+
+    two_copy.wait_recv()
+    gain_two_row = gain[1:2, :]
+    step = 32
+
+    def residual(block, acc):
+        at = pl.ds(pl.multiple_of(block * step, step), step)
+        back = part_two[at, :] + recv_two[at, :].astype(jnp.float32)
+        value = resid[at, :]
+        scale = norm_scale(value)
+        grad = grad_all[at, :].astype(jnp.float32) + norm_back(value, scale, gain_two_row, back)
+        grad_resid[at, :] = grad
+        grad_o[at, :] = grad.astype(jnp.bfloat16)
+        return acc + jnp.sum(back * value * scale, axis=0, keepdims=True)
+
+    gain_two = lax.fori_loop(0, group // step, residual, jnp.zeros((1, resid.shape[1]), jnp.float32))
+    small_send[0] = jnp.zeros(small_send.shape[1:], jnp.float32)
+    small_send[0, 1:2, :] = gain_two
+
+    keep_one = masks[:, 0:1]
+    keep_two = masks[:, 1:2]
+    grad_mix = jnp.dot(grad_o[...], out_w[...], preferred_element_type=jnp.float32)
+    grad_proj[:, chans : 2 * chans] = (grad_mix * conv[...]).astype(jnp.bfloat16)
+    grad_conv = grad_mix * cgate[...]
+    lead_one = keep_one * grad_conv
+    lead_two = keep_two * grad_conv
+    head[...] = jnp.zeros_like(head)
+    head[0:1, :] = taps[0:1, :] * lead_two[0:1, :]
+    head[1:2, :] = taps[1:2, :] * lead_one[0:1, :] + taps[0:1, :] * lead_two[1:2, :]
+    head_copy.start()
+    lead_one_ref[...] = lead_one
+    lead_two_ref[...] = lead_two
+    gconv_ref[...] = grad_conv
+    block = group
+
+    def out_block(zz, carry):
+        at = pl.ds(pl.multiple_of(zz * block, block), block)
+        value = contract_rows(grad_o[:, at], mixed_in[...])
+        term_out[zz] = value.astype(jnp.bfloat16).reshape(term_out.shape[1:])
+        return carry
+
+    lax.fori_loop(0, DEPTH, out_block, 0)
+    out_piece = ready
+    core_copy(out_piece).start()
+    after_y(0)
+    after_y(1)
+
+    head_copy.wait_recv()
+    lead_one = lead_one_ref[...]
+    lead_two = lead_two_ref[...]
+    grad_conv = gconv_ref[...]
+    row_ids = lax.broadcasted_iota(jnp.int32, (group, chans), 0)
+    moved_one = jnp.where(row_ids < group - 1, pltpu.roll(lead_one, group - 1, 0), 0.0)
+    moved_two = jnp.where(row_ids < group - 2, pltpu.roll(lead_two, group - 2, 0), 0.0)
+    border = masks[:, 2:3] * after[0:1, :] + masks[:, 3:4] * after[1:2, :]
+    border = jnp.where(here == total_seq - 1, jnp.zeros_like(border), border)
+    grad_gated = taps[2:3, :] * grad_conv + taps[1:2, :] * moved_one + taps[0:1, :] * moved_two + border
+    grad_proj[:, :chans] = (grad_gated * xin[...]).astype(jnp.bfloat16)
+    grad_proj[:, 2 * chans :] = (grad_gated * bgate[...]).astype(jnp.bfloat16)
+    part_one[...] = contract_cols(grad_proj[...], in_w[...])
+    send_one[...] = part_one[pl.ds(pl.multiple_of((1 - part) * rows, rows), rows), :].astype(jnp.bfloat16)
+    one_copy.start()
+
+    def in_block(zz, carry):
+        at = pl.ds(pl.multiple_of(zz * block, block), block)
+        value = contract_rows(mixer[:, at], grad_proj[...])
+        term_in[zz] = value.astype(jnp.bfloat16).reshape(term_in.shape[1:])
+        return carry
+
+    lax.fori_loop(0, DEPTH, in_block, 0)
+    for piece in range(ready + 1, count):
+        core_copy(piece).start()
+    small_send[0, 2:3, :chans] = jnp.sum(lead_two * two_back[...], axis=0, keepdims=True)
+    small_send[0, 3:4, :chans] = jnp.sum(lead_one * one_back[...], axis=0, keepdims=True)
+    small_send[0, 4:5, :chans] = jnp.sum(grad_conv * current[...].astype(jnp.float32), axis=0, keepdims=True)
+    after_core(ready)
+    after_y(2)
+    for piece in range(ready + 1, count):
+        after_core(piece)
+    after_y(3)
+    after_z(0)
+
+    one_copy.wait_recv()
+    mine = pl.ds(pl.multiple_of(part * rows, rows), rows)
+    back_one = part_one[mine, :] + recv_one[...].astype(jnp.float32)
+    own_tokens = tokens[mine, :].astype(jnp.float32)
+    scale_one = norm_scale(own_tokens)
+    grad_input[...] = (
+        grad_resid[mine, :] + norm_back(own_tokens, scale_one, gain[0:1, :], back_one)
+    ).astype(jnp.bfloat16)
+    small_send[0, 0:1, :] = jnp.sum(back_one * own_tokens * scale_one, axis=0, keepdims=True)
+
+    s_core = remote(small_send.at[0], small_core, s_send.at[0], s_recv.at[0], other_core)
+    s_y = remote(small_send.at[1], small_y, s_send.at[1], s_recv.at[1], y_partner)
+    s_z = [
+        remote(small_send.at[2], small_z.at[k - 1], s_send.at[1 + k], s_recv.at[1 + k], z_partners[k])
+        for k in range(1, DEPTH)
+    ]
+    s_x = remote(small_send.at[3], small_x, s_send.at[5], s_recv.at[5], x_partner)
+    s_core.start()
+    after_y(4)
+    after_z(1)
+    s_core.wait_recv()
+    small_send[1] = small_send[0] + small_core[...]
+    s_y.start()
+    after_y(5)
+    after_z(2)
+    s_y.wait_recv()
+    small_send[2] = small_send[1] + small_y[...]
+    for copy in s_z:
+        copy.start()
+    after_y(6)
+    after_z(3)
+    for copy in s_z:
+        copy.wait_recv()
+    small_send[3] = small_send[2] + small_z[0] + small_z[1] + small_z[2]
+    s_x.start()
+    for piece in range(7, count):
+        after_y(piece)
+        after_z(piece - 3)
+    s_x.wait_recv()
+    first = lax.broadcasted_iota(jnp.int32, small.shape, 0) == 0
+    small[...] = small_send[3] + jnp.where(first, small_x[...], 0.0)
+    for piece in range(count - 3, count):
+        after_z(piece)
+    for copy in [two_copy, one_copy, head_copy, s_core, s_y, *s_z, s_x]:
+        copy.wait_send()
+    for piece in range(count):
+        core_copy(piece).wait_send()
+        y_copy(piece).wait_send()
+        for k in range(1, DEPTH):
+            z_copy(piece, k).wait_send()
+
+
+def mixer_back(term_gu, term_down, values, seq):
+    tall = seq // (DEPTH * CORES)
+    group, width = values[1].shape
+    chans = values[6].shape[1]
+    depth = width // seq
+    bf, fl = jnp.bfloat16, jnp.float32
+    widths = [term_gu.shape[1], term_down.shape[1], chans, 3 * chans]
+    pieces = pieces_of(widths, 768)
+    ready = sum(1 for piece in pieces if piece[0] < 2)
+    count = len(pieces)
+    lead = (DEPTH, tall)
+    dma = pltpu.SemaphoreType.DMA
+    vmem = pltpu.VMEM
+    in_vmem = pl.BlockSpec(memory_space=pltpu.VMEM)
+    small = (8, width)
+    big = [t.reshape((DEPTH, tall, CORES, depth, t.shape[1])) for t in (term_gu, term_down)]
+    return pl.pallas_call(
+        functools.partial(mixer_back_kernel, pieces, ready),
+        out_shape=[jax.ShapeDtypeStruct((depth, w), fl) for w in widths]
+        + [jax.ShapeDtypeStruct((group // 2, width), bf), jax.ShapeDtypeStruct(small, fl)],
+        in_specs=[pl.BlockSpec(memory_space=pl.ANY)] * 2 + [in_vmem] * len(values),
+        out_specs=[in_vmem] * 6,
+        scratch_shapes=[vmem(lead + (depth, w), bf) for w in widths[:2]]
+        + [vmem(lead + (CORES, depth, w), bf) for w in widths[2:]]
+        + [vmem(lead + (depth, w), bf) for w in widths]
+        + [vmem((DEPTH, depth, w), bf) for w in widths]
+        + [vmem((DEPTH - 1, depth, w), bf) for w in widths]
+        + [
+            vmem((group, width), bf),
+            vmem((group, width), fl),
+            vmem((group, width), bf),
+            vmem((group, 3 * chans), bf),
+            vmem((group, width), fl),
+            vmem((group // 2, width), bf),
+            vmem((group // 2, width), bf),
+            vmem((8, chans), fl),
+            vmem((8, chans), fl),
+            vmem((group, chans), fl),
+            vmem((group, chans), fl),
+            vmem((group, chans), fl),
+            vmem((4,) + small, fl),
+            vmem(small, fl),
+            vmem(small, fl),
+            vmem((DEPTH - 1,) + small, fl),
+            vmem(small, fl),
+            dma((count,)),
+            dma((count,)),
+            dma((count,)),
+            dma((count,)),
+            dma((count,)),
+            dma((count, DEPTH)),
+            dma((count, DEPTH)),
+            dma((2,)),
+            dma((2,)),
+            dma((2,)),
+            dma((6,)),
+            dma((6,)),
+        ],
+        compiler_params=pltpu.CompilerParams(
+            collective_id=2, has_side_effects=True, vmem_limit_bytes=60 * 1024 * 1024
+        ),
+        name="mixer_backward",
+    )(*big, *values)
+
+
 def mp_gather(value, axis):
     if lax.axis_size("mp") != 2:
         return lax.all_gather(value, "mp", axis=axis, tiled=True)
@@ -527,7 +842,57 @@
     )
     term_down = contract_rows(grad_all, hidden).astype(jnp.bfloat16)
     term_gu = contract_rows(ff_all, grad_both).astype(jnp.bfloat16)
-    back_two = mp_sum(contract_cols(grad_both, gu_flat))
+    partial_two = contract_cols(grad_both, gu_flat)
+    if wide == 2 and seq == DEPTH * 2 * CORES:
+        row_ids = jnp.arange(group, dtype=jnp.int32)[:, None]
+        masks = jnp.concatenate(
+            [
+                keep_one,
+                keep_two,
+                (row_ids == count - 2).astype(jnp.float32),
+                (row_ids == count - 1).astype(jnp.float32),
+            ],
+            axis=1,
+        )
+        sum_gu, sum_down, sum_out, sum_in, grad_input, small_sums = mixer_back(
+            term_gu,
+            term_down,
+            [
+                partial_two.astype(jnp.bfloat16),
+                partial_two,
+                resid,
+                grad_all,
+                whole_rows[0].reshape(group, width),
+                mixer_all,
+                mixed_in,
+                conv,
+                cgate,
+                xin,
+                bgate,
+                gated,
+                one_back,
+                two_back,
+                masks,
+                out_turned,
+                in_flat,
+                gain_all,
+                conv_taps,
+            ],
+            seq,
+        )
+        here = lax.axis_index("seq")
+        gain_size = gains.shape[1]
+        return (
+            mixed,
+            grad_input,
+            lax.dynamic_slice(small_sums, (0, (here * wide + mp_place) * gain_size), (2, gain_size)),
+            sum_in.reshape(depth, 3, chans),
+            sum_out.T,
+            sum_gu.reshape(depth, 2, units),
+            sum_down.T,
+            lax.dynamic_slice(small_sums, (2, here * tap_cols), (3, tap_cols)),
+        )
+    back_two = mp_sum(partial_two)
     grad_resid = grad_all.astype(jnp.float32) + norm_back(resid, scale_two, gain_all[1], back_two)
     gain_two = jnp.sum(own(back_two * resid * scale_two), axis=0)
     grad_o_all = grad_resid.astype(jnp.bfloat16)

time: 358 us -> 379 us (1.059)
  Pallas kernels: 252 us -> 300 us
  waiting for transfers between devices: 21.5 us -> 11.9 us
  matrix products: 36 us -> 28.9 us
  other arithmetic: 16 us -> 9.21 us
  starting transfers between devices: 10.6 us -> 6.04 us
    pallas_call x1, Pallas kernels: 128 us -> 176 us  [mixer_back(): pl.pallas_call(functools.partial(mixer_back_kernel, pieces, ready), out_s...]
    ppermute x2 -> x1, waiting for transfers between devices: 5.96 us -> 0.01 us  [mp_sum_own(): other = lax.ppermute(sent, 'mp', [(0, 1), (1, 0)])]
    dot_general x4 -> x2, matrix products: 13.2 us -> 9.1 us  [contract_rows(): lax.dot_general(left, right, (((0,), (0,)), ((), ())), preferred_element_...]
    ppermute x2 -> x1, waiting for transfers between devices: 15.2 us -> 11.4 us  [mp_sum(): other = lax.ppermute(value.astype(jnp.bfloat16), 'mp', [(0, 1), (1, 0)])]
    dot_general x4 -> x3, matrix products: 11.1 us -> 8.99 us  [contract_cols(): lax.dot_general(left, right, (((1,), (1,)), ((), ())), preferred_element_...]
  transfers between devices with their start and end apart: 8 -> 4, of which waited for: 4 -> 2; matrix products, arithmetic and copies ran while one was open for 10% -> 5% of each run, Pallas kernels for 0% -> 47%
where the time goes in v2:
time: 379 us; the launch traced here: 377 us
  Pallas kernels  300 us (79%)
  matrix products  28.9 us (8%)
  local copies, waits for them, and re-layouts  19.1 us (5%)
  waiting for transfers between devices  11.9 us (3%)
  other arithmetic  9.21 us (2%)
  starting transfers between devices  6.04 us (2%)
    pallas_call x1, Pallas kernels, mixer_back(): pl.pallas_call(functools.partial(mixer_back_kernel, pieces, ready), out_s...  176 us
    pallas_call x1, Pallas kernels, gather_all(): pl.pallas_call(functools.partial(gather_kernel, pieces, len(shards), halv...  124 us
    ppermute x1, waiting for transfers between devices, mp_sum(): other = lax.ppermute(value.astype(jnp.bfloat16), 'mp', [(0, 1), (1, 0)])  11.4 us
    dot_general x2, matrix products, contract_rows(): lax.dot_general(left, right, (((0,), (0,)), ((), ())), preferred_element_...  9.1 us
    dot_general x3, matrix products, contract_cols(): lax.dot_general(left, right, (((1,), (1,)), ((), ())), preferred_element_...  8.99 us
  transfers between devices with their start and end apart: 4, of which 2 were waited for; matrix products, arithmetic and copies ran while one was open for 5% of the time, Pallas kernels for 47%

profile of v2, /device:TPU:0, one launch (start us, length us, event | category | flops | bytes accessed | tf_op | source)
XLA Modules:
  0.0 376.9 jit_solution(10651453578600882038)
XLA Ops:
  0.6 3.0 collective-permute-start
  4.3 0.7 compare_convert_fusion.3
  5.0 1.6 copy.36
  6.6 1.9 copy.37
  9.3 1.5 scatter.9.refs_0_
  11.5 124.3 %gather_weights.1 = (bf16[4,2,2,16,128]{4,3,2,1,0:T(8,128)(2,1)}, bf16[4,2,2,64,1536]{4,3,2,1,0:T(8,128)(2,1)}, bf16[4,2,2,64,512]{4,3,2,1,0:T(8,128)(2,1)}, bf1...) custom-call(bf16[16,128]{1,0:T(8,128)(2,1)} %copy-done.11, ...), custom_call_target="tpu_custom_call" | custom-call | bytes 294649856 | tf_op jit(solution)/shard_map/gather_weights/pallas_call | solution.py:241
  135.8 0.9 bitcast_convert_fusion
  136.7 1.2 fusion.4
  138.0 1.2 fusion.6
  139.3 2.9 fusion.21
  142.2 2.4 collective-permute-start.1
  145.6 2.0 multiply_convert_fusion.4
  147.6 1.4 fusion.19
  149.3 0.8 copy.31.refs_16_
  150.8 0.7 reshape.219.refs_20_
  151.8 11.4 %collective-permute-done.2 = bf16[256,1024]{1,0:T(8,128)(2,1)S(1)} collective-permute-done((bf16[256,1024]{1,0:T(8,128)(2,1)S(1)}, bf16[256,1024]{1,0:T(8,128)(2,1)S(1)}, u32[]{:S(2)}, u32[]{:S(2)}) %collective-permute-start.2) | collective-permute-done | bytes 524320 | tf_op jit(solution)/shard_map/ppermute | solution.py:749
  163.2 1.3 multiply_reduce_fusion
  164.5 6.0 %fusion.16 = f32[256,4608]{1,0:T(8,128)S(1)} fusion(bf16[1024,4608]{1,0:T(8,128)(2,1)} %bitcast.82, f32[256,1024]{1,0:T(8,128)S(1)} %get-tuple-element.83.refs_4_, f32[1024]{0:T(1024)S(1)} %mul.168, f32[256]{0:T(256)S(1)} %add_rsqrt_fusion), kind=kOutput, calls=%fused_computation.57 | convolution fusion | flops 2416705536 | bytes 15209472 | tf_op jit(solution)/shard_map/dot_general | solution.py:829
  170.6 1.9 multiply_convert_fusion.1
  172.6 3.8 %fusion.20 = (bf16[256,1024]{1,0:T(8,128)(2,1)}, f32[256,1024]{1,0:T(8,128)}) fusion(bf16[1024,4608]{1,0:T(8,128)(2,1)S(1)} %bitcast.85, bf16[256,2304]{1,0:T(8,128)(2,1)S(1)} %get-tuple-element.87, bf16[256,2304]{1,0:T(8,128)(2,1)S(1)} %get-tuple-element.86), kind=kOutput, calls=%fused_computation.61 | convolution fusion | flops 2420899840 | bytes 13369344 | tf_op jit(solution)/shard_map/dot_general | solution.py:25
  176.4 5.4 %convolution_convert_fusion = bf16[1024,4608]{1,0:T(8,128)(2,1)} fusion(bf16[256,2304]{1,0:T(8,128)(2,1)S(1)} %get-tuple-element.87, bf16[256,2304]{1,0:T(8,128)(2,1)S(1)} %get-tuple-element.86, f32[256,1024]{1,0:T(8,128)S(1)} %get-tuple-element.83.refs_4_, f32[1024]{0:T(1024)S(1)} %mul.168, f32[256]{0:T(256)S(1)} %add_rsqrt_fusion), kind=kOutput, calls=%fused_computation | convolution fusion | flops 2426142720 | bytes 12850176 | tf_op jit(solution)/shard_map/dot_general | solution.py:19
  181.8 3.7 fusion.22
  186.0 3.7 convolution_convert_fusion.1
  189.6 175.7 %mixer_backward.1 = (f32[64,4608]{1,0:T(8,128)}, f32[64,2304]{1,0:T(8,128)}, f32[64,512]{1,0:T(8,128)}, f32[64,1536]{1,0:T(8,128)}, bf16[128,1024]{1,0:T(8,128)(2,1)}, /*index=5*/f32[8,1024]{1,0:T(8,128)}) custom-call(bf16[4,2,2,64,4608]{4,3,2,1,0:T(8,128)(2,1)} %bitcast.57, bf16[4,2,2,64,2304]{4,3,2,1,0:T(8,128)(2,1)} %bitcast.58, ...), custom_call_target="tpu_custom_call" | custom-call | tf_op jit(solution)/shard_map/mixer_backward/pallas_call | solution.py:687
  365.4 1.9 copy.41
  367.3 3.1 reshape.221
  370.4 1.3 constant_dynamic-slice_fusion
  371.7 1.3 constant_dynamic-slice_fusion.2
  373.0 0.8 select_convert_fusion
  373.8 0.7 copy.49
  374.5 1.6 copy.50
  376.1 0.8 copy.51
  (68 shorter events, 4.2 us)
Async XLA Ops:
  0.6 8.0 %collective-permute-start = (bf16[2,32]{1,0:T(2,128)(2,1)}, bf16[2,32]{1,0:T(2,128)(2,1)S(1)}, u32[]{:S(2)}, u32[]{:S(2)}) collective-permute-start(bf16[2,32]{1,0:T(2,128)(2,1)} %param.18), channel_id=1, source_target_pairs={{0,1},{1,0},{2,3},{3,2},{4,5},{5,4},{6,7},{7,6},{8,9},{9,8},{10,11... | collective-permute-start | bytes 392 | tf_op jit(solution)/shard_map/ppermute | solution.py:739
  10.9 0.6 copy-start.11
  142.2 5.3 %copy-start.6 = (bf16[256,512]{1,0:T(8,128)(2,1)}, bf16[256,512]{1,0:T(8,128)(2,1)S(1)}, u32[]{:S(2)}) copy-start(bf16[256,512]{1,0:T(8,128)(2,1)S(1)} %multiply_convert_fusion.5.refs_13_) | copy-start | bytes 786436
  142.2 3.3 collective-permute-start.1
  145.6 2.0 copy-start.4
  147.5 4.3 %copy-start.7 = (bf16[256,512]{1,0:T(8,128)(2,1)}, bf16[256,512]{1,0:T(8,128)(2,1)S(1)}, u32[]{:S(2)}) copy-start(bf16[256,512]{1,0:T(8,128)(2,1)S(1)} %get-tuple-element.84.refs_8_) | copy-start | bytes 786436
  147.6 4.0 %copy-start.8 = (bf16[2,128,1024]{2,1,0:T(8,128)(2,1)S(1)}, bf16[2,128,1024]{2,1,0:T(8,128)(2,1)}, u32[]{:S(2)}) copy-start(bf16[2,128,1024]{2,1,0:T(8,128)(2,1)} %get-tuple-element.51) | copy-start | bytes 1572868
  147.6 15.6 %copy-start.2 = (bf16[2,128,1024]{2,1,0:T(8,128)(2,1)S(1)}, bf16[2,128,1024]{2,1,0:T(8,128)(2,1)}, u32[]{:S(2)}) copy-start(bf16[2,128,1024]{2,1,0:T(8,128)(2,1)} %get-tuple-element.45) | copy-start | bytes 1572868
  149.0 14.2 %copy-start.5 = (f32[256,1024]{1,0:T(8,128)S(1)}, f32[256,1024]{1,0:T(8,128)}, u32[]{:S(2)}) copy-start(f32[256,1024]{1,0:T(8,128)} %get-tuple-element.107) | copy-start | bytes 3145732
  149.0 14.2 %collective-permute-start.2 = (bf16[256,1024]{1,0:T(8,128)(2,1)S(1)}, bf16[256,1024]{1,0:T(8,128)(2,1)S(1)}, u32[]{:S(2)}, u32[]{:S(2)}) collective-permute-start(bf16[256,1024]{1,0:T(8,128)(2,1)S(1)} %get-tuple-element.106), channel_id=1, source_target_pairs={{0,1},{1,0},{2,3},{3,2},{4,5},{5,4},{6,7},{7,6},{8,9},{9,8},{10,11... | collective-permute-start | bytes 1572872 | tf_op jit(solution)/shard_map/ppermute | solution.py:749
  151.7 34.3 %copy-start.3 = (bf16[256,1024]{1,0:T(8,128)(2,1)}, bf16[256,1024]{1,0:T(8,128)(2,1)S(1)}, u32[]{:S(2)}) copy-start(bf16[256,1024]{1,0:T(8,128)(2,1)S(1)} %bitcast_select_fusion.refs_5_) | copy-start | bytes 1572868
  163.2 7.4 %slice-start.3 = ((s8[4718592]{0:T(1024)(128)(4,1)}), s8[4194304]{0:T(1024)(128)(4,1)S(1)}, s32[]{:S(2)}) async-start(s8[4718592]{0:T(1024)(128)(4,1)} %bitcast.87), calls=%async_computation.3 | async-start | bytes 8388608
  164.5 11.9 %copy-start = (f32[256,1024]{1,0:T(8,128)}, f32[256,1024]{1,0:T(8,128)S(1)}, u32[]{:S(2)}) copy-start(f32[256,1024]{1,0:T(8,128)S(1)} %get-tuple-element.83.refs_4_) | copy-start | bytes 3145732
  164.5 6.1 %slice-start.4 = ((s8[4718592]{0:T(1024)(128)(4,1)}), s8[524288]{0:T(1024)(128)(4,1)S(1)}, s32[]{:S(2)}) async-start(s8[4718592]{0:T(1024)(128)(4,1)} %bitcast.87), calls=%async_computation.4 | async-start | bytes 1048576
  164.5 8.0 %slice-start = ((s8[9437184]{0:T(1024)(128)(4,1)}), s8[4194304]{0:T(1024)(128)(4,1)S(1)}, s32[]{:S(2)}) async-start(s8[9437184]{0:T(1024)(128)(4,1)} %bitcast.83), calls=%async_computation | async-start | bytes 8388608
  164.5 8.0 %slice-start.1 = ((s8[9437184]{0:T(1024)(128)(4,1)}), s8[4194304]{0:T(1024)(128)(4,1)S(1)}, s32[]{:S(2)}) async-start(s8[9437184]{0:T(1024)(128)(4,1)} %bitcast.83), calls=%async_computation.1 | async-start | bytes 8388608
  170.6 1.9 slice-start.2
  185.6 187.4 %collective-permute-start.3 = (bf16[128,1024]{1,0:T(8,128)(2,1)S(1)}, bf16[128,1024]{1,0:T(8,128)(2,1)S(1)}, u32[]{:S(2)}, u32[]{:S(2)}) collective-permute-start(bf16[128,1024]{1,0:T(8,128)(2,1)S(1)} %dynamic-slice_convert_fusion), channel_id=1, source_target_pairs={{0,1},{1,0},{2,3},{3,2},{4,5},{5,4},{6,7},{7,6},{8,9},{9,8},{10,11... | collective-permute-start | bytes 786440 | tf_op jit(solution)/shard_map/ppermute | solution.py:758
  365.4 7.7 %copy-start.1 = (f32[256,1024]{1,0:T(8,128)S(1)}, f32[256,1024]{1,0:T(8,128)}, u32[]{:S(2)}) copy-start(f32[256,1024]{1,0:T(8,128)} %copy-done) | copy-start | bytes 3145732
  365.4 8.5 %copy-start.10 = (bf16[128,1024]{1,0:T(8,128)(2,1)S(1)}, bf16[128,1024]{1,0:T(8,128)(2,1)}, u32[]{:S(2)}) copy-start(bf16[128,1024]{1,0:T(8,128)(2,1)} %get-tuple-element.121) | copy-start | bytes 786436
  367.3 8.9 %copy-start.9 = (f32[64,2304]{1,0:T(8,128)S(1)}, f32[64,2304]{1,0:T(8,128)}, u32[]{:S(2)}) copy-start(f32[64,2304]{1,0:T(8,128)} %get-tuple-element.57) | copy-start | bytes 1769476

commit v3 on v2

--- a/solution.py
+++ b/solution.py
@@ -141,7 +141,7 @@
             )
         )
 
-    for piece in range(len(pieces)):
+    def send_z(piece):
         for k in range(1, DEPTH):
             begin(
                 remote(
@@ -152,6 +152,11 @@
                     z_partners[k],
                 )
             )
+
+    ahead = 3
+    for piece in range(min(ahead, len(pieces))):
+        send_z(piece)
+    for piece in range(len(pieces)):
         send_y(piece, 0)
         if piece == 0:
             for index in range(halves):
@@ -189,6 +194,8 @@
             ).wait_recv()
             send_y(piece, k)
             send_core(piece, k, 0)
+        if piece + ahead < len(pieces):
+            send_z(piece + ahead)
 
     def from_y(piece):
         for k in range(DEPTH):
@@ -233,7 +240,7 @@
 
 def gather_all(shards, row_parts, seq, wide):
     tall = seq // (DEPTH * CORES)
-    pieces = pieces_of([shard.shape[1] for shard in shards], 1536)
+    pieces = pieces_of([shard.shape[1] for shard in shards], 768)
     count = len(pieces)
     moved = sum(shard.size * shard.dtype.itemsize for shard in shards) * seq
     dma = pltpu.SemaphoreType.DMA
@@ -528,12 +535,28 @@
     head_copy = remote(head, after, h_sem.at[0], h_sem.at[1], earlier)
 
     count = len(pieces)
+    ahead = 3
+
+    def begin_core(piece):
+        core_copy(piece).start()
+        if piece < ready:
+            own_copy(piece).start()
+
+    def turn(piece):
+        if piece < count:
+            after_core(piece)
+            if piece + ahead < ready:
+                begin_core(piece + ahead)
+        if 0 <= piece - 2 < count:
+            after_y(piece - 2)
+        if 0 <= piece - 4 < count:
+            after_z(piece - 4)
+
     two_copy.start()
-    for piece in range(ready):
-        core_copy(piece).start()
-        own_copy(piece).start()
-    for piece in range(ready):
-        after_core(piece)
+    for piece in range(ahead):
+        begin_core(piece)
+    turn(0)
+    turn(1)
 
     two_copy.wait_recv()
     gain_two_row = gain[1:2, :]
@@ -552,6 +575,8 @@
     gain_two = lax.fori_loop(0, group // step, residual, jnp.zeros((1, resid.shape[1]), jnp.float32))
     small_send[0] = jnp.zeros(small_send.shape[1:], jnp.float32)
     small_send[0, 1:2, :] = gain_two
+
+    turn(2)
 
     keep_one = masks[:, 0:1]
     keep_two = masks[:, 1:2]
@@ -567,6 +592,7 @@
     lead_one_ref[...] = lead_one
     lead_two_ref[...] = lead_two
     gconv_ref[...] = grad_conv
+    turn(3)
     block = group
 
     def out_block(zz, carry):
@@ -576,10 +602,8 @@
         return carry
 
     lax.fori_loop(0, DEPTH, out_block, 0)
-    out_piece = ready
-    core_copy(out_piece).start()
-    after_y(0)
-    after_y(1)
+    turn(4)
+    begin_core(ready)
 
     head_copy.wait_recv()
     lead_one = lead_one_ref[...]
@@ -597,6 +621,8 @@
     send_one[...] = part_one[pl.ds(pl.multiple_of((1 - part) * rows, rows), rows), :].astype(jnp.bfloat16)
     one_copy.start()
 
+    turn(5)
+
     def in_block(zz, carry):
         at = pl.ds(pl.multiple_of(zz * block, block), block)
         value = contract_rows(mixer[:, at], grad_proj[...])
@@ -605,16 +631,11 @@
 
     lax.fori_loop(0, DEPTH, in_block, 0)
     for piece in range(ready + 1, count):
-        core_copy(piece).start()
+        begin_core(piece)
+    turn(6)
     small_send[0, 2:3, :chans] = jnp.sum(lead_two * two_back[...], axis=0, keepdims=True)
     small_send[0, 3:4, :chans] = jnp.sum(lead_one * one_back[...], axis=0, keepdims=True)
     small_send[0, 4:5, :chans] = jnp.sum(grad_conv * current[...].astype(jnp.float32), axis=0, keepdims=True)
-    after_core(ready)
-    after_y(2)
-    for piece in range(ready + 1, count):
-        after_core(piece)
-    after_y(3)
-    after_z(0)
 
     one_copy.wait_recv()
     mine = pl.ds(pl.multiple_of(part * rows, rows), rows)
@@ -634,31 +655,26 @@
     ]
     s_x = remote(small_send.at[3], small_x, s_send.at[5], s_recv.at[5], x_partner)
     s_core.start()
-    after_y(4)
-    after_z(1)
+    turn(7)
     s_core.wait_recv()
     small_send[1] = small_send[0] + small_core[...]
     s_y.start()
-    after_y(5)
-    after_z(2)
+    turn(8)
     s_y.wait_recv()
     small_send[2] = small_send[1] + small_y[...]
     for copy in s_z:
         copy.start()
-    after_y(6)
-    after_z(3)
+    turn(9)
     for copy in s_z:
         copy.wait_recv()
     small_send[3] = small_send[2] + small_z[0] + small_z[1] + small_z[2]
     s_x.start()
-    for piece in range(7, count):
-        after_y(piece)
-        after_z(piece - 3)
+    turn(10)
     s_x.wait_recv()
     first = lax.broadcasted_iota(jnp.int32, small.shape, 0) == 0
     small[...] = small_send[3] + jnp.where(first, small_x[...], 0.0)
-    for piece in range(count - 3, count):
-        after_z(piece)
+    for piece in range(11, count + 4):
+        turn(piece)
     for copy in [two_copy, one_copy, head_copy, s_core, s_y, *s_z, s_x]:
         copy.wait_send()
     for piece in range(count):
@@ -666,7 +682,6 @@
         y_copy(piece).wait_send()
         for k in range(1, DEPTH):
             z_copy(piece, k).wait_send()
-
 
 def mixer_back(term_gu, term_down, values, seq):
     tall = seq // (DEPTH * CORES)

time: 379 us -> 328 us (0.87)
  Pallas kernels: 300 us -> 250 us
    pallas_call x1, Pallas kernels: 176 us -> 135 us  [mixer_back(): pl.pallas_call(functools.partial(mixer_back_kernel, pieces, ready), out_s...]
    pallas_call x1, Pallas kernels: 124 us -> 115 us  [gather_all(): pl.pallas_call(functools.partial(gather_kernel, pieces, len(shards), halv...]
  transfers between devices with their start and end apart: 4 -> 4, of which waited for: 2 -> 2; matrix products, arithmetic and copies ran while one was open for 5% -> 6% of each run, Pallas kernels for 47% -> 41%
where the time goes in v3:
time: 328 us; the launch traced here: 327 us
  Pallas kernels  250 us (76%)
  matrix products  28.9 us (9%)
  local copies, waits for them, and re-layouts  19.1 us (6%)
  waiting for transfers between devices  11.6 us (4%)
  other arithmetic  9.21 us (3%)
  starting transfers between devices  6.8 us (2%)
    pallas_call x1, Pallas kernels, mixer_back(): pl.pallas_call(functools.partial(mixer_back_kernel, pieces, ready), out_s...  135 us
    pallas_call x1, Pallas kernels, gather_all(): pl.pallas_call(functools.partial(gather_kernel, pieces, len(shards), halv...  115 us
    ppermute x1, waiting for transfers between devices, mp_sum(): other = lax.ppermute(value.astype(jnp.bfloat16), 'mp', [(0, 1), (1, 0)])  11 us
    dot_general x2, matrix products, contract_rows(): lax.dot_general(left, right, (((0,), (0,)), ((), ())), preferred_element_...  9.1 us
    dot_general x3, matrix products, contract_cols(): lax.dot_general(left, right, (((1,), (1,)), ((), ())), preferred_element_...  8.99 us
  transfers between devices with their start and end apart: 4, of which 2 were waited for; matrix products, arithmetic and copies ran while one was open for 6% of the time, Pallas kernels for 41%

profile of v3, /device:TPU:0, one launch (start us, length us, event | category | flops | bytes accessed | tf_op | source)
XLA Modules:
  0.0 327.3 jit_solution(5171542292200242997)
XLA Ops:
  0.6 3.0 collective-permute-start
  4.3 0.7 compare_convert_fusion.3
  5.0 1.6 copy.36
  6.6 1.9 copy.37
  9.3 1.5 scatter.9.refs_0_
  11.5 115.3 %gather_weights.1 = (bf16[4,2,2,16,128]{4,3,2,1,0:T(8,128)(2,1)}, bf16[4,2,2,64,1536]{4,3,2,1,0:T(8,128)(2,1)}, bf16[4,2,2,64,512]{4,3,2,1,0:T(8,128)(2,1)}, bf1...) custom-call(bf16[16,128]{1,0:T(8,128)(2,1)} %copy-done.11, ...), custom_call_target="tpu_custom_call" | custom-call | bytes 294649856 | tf_op jit(solution)/shard_map/gather_weights/pallas_call | solution.py:248
  126.8 0.9 bitcast_convert_fusion
  127.7 1.2 fusion.4
  129.0 1.2 fusion.6
  130.2 2.9 fusion.21
  133.2 2.6 collective-permute-start.1
  136.7 2.0 multiply_convert_fusion.4
  138.7 1.4 fusion.19
  140.7 0.8 copy.31.refs_16_
  142.3 0.7 reshape.219.refs_20_
  143.3 11.0 %collective-permute-done.2 = bf16[256,1024]{1,0:T(8,128)(2,1)S(1)} collective-permute-done((bf16[256,1024]{1,0:T(8,128)(2,1)S(1)}, bf16[256,1024]{1,0:T(8,128)(2,1)S(1)}, u32[]{:S(2)}, u32[]{:S(2)}) %collective-permute-start.2) | collective-permute-done | bytes 524320 | tf_op jit(solution)/shard_map/ppermute | solution.py:764
  154.3 1.3 multiply_reduce_fusion
  155.6 6.0 %fusion.16 = f32[256,4608]{1,0:T(8,128)S(1)} fusion(bf16[1024,4608]{1,0:T(8,128)(2,1)} %bitcast.82, f32[256,1024]{1,0:T(8,128)S(1)} %get-tuple-element.83.refs_4_, f32[1024]{0:T(1024)S(1)} %mul.168, f32[256]{0:T(256)S(1)} %add_rsqrt_fusion), kind=kOutput, calls=%fused_computation.57 | convolution fusion | flops 2416705536 | bytes 15209472 | tf_op jit(solution)/shard_map/dot_general | solution.py:844
  161.7 1.9 multiply_convert_fusion.1
  163.7 3.8 %fusion.20 = (bf16[256,1024]{1,0:T(8,128)(2,1)}, f32[256,1024]{1,0:T(8,128)}) fusion(bf16[1024,4608]{1,0:T(8,128)(2,1)S(1)} %bitcast.85, bf16[256,2304]{1,0:T(8,128)(2,1)S(1)} %get-tuple-element.87, bf16[256,2304]{1,0:T(8,128)(2,1)S(1)} %get-tuple-element.86), kind=kOutput, calls=%fused_computation.61 | convolution fusion | flops 2420899840 | bytes 13369344 | tf_op jit(solution)/shard_map/dot_general | solution.py:25
  167.5 5.4 %convolution_convert_fusion = bf16[1024,4608]{1,0:T(8,128)(2,1)} fusion(bf16[256,2304]{1,0:T(8,128)(2,1)S(1)} %get-tuple-element.87, bf16[256,2304]{1,0:T(8,128)(2,1)S(1)} %get-tuple-element.86, f32[256,1024]{1,0:T(8,128)S(1)} %get-tuple-element.83.refs_4_, f32[1024]{0:T(1024)S(1)} %mul.168, f32[256]{0:T(256)S(1)} %add_rsqrt_fusion), kind=kOutput, calls=%fused_computation | convolution fusion | flops 2426142720 | bytes 12850176 | tf_op jit(solution)/shard_map/dot_general | solution.py:19
  172.9 3.7 %fusion.22 = f32[256,1024]{1,0:T(8,128)S(1)} fusion(bf16[256,2304]{1,0:T(8,128)(2,1)S(1)} %get-tuple-element.88, bf16[1024,2304]{1,0:T(8,128)(2,1)} %bitcast.86), kind=kOutput, calls=%fused_computation.63 | convolution fusion | flops 1207959552 | bytes 6946816 | tf_op jit(solution)/shard_map/dot_general | solution.py:25
  177.4 3.7 %convolution_convert_fusion.1 = bf16[1024,2304]{1,0:T(8,128)(2,1)} fusion(bf16[256,1024]{1,0:T(8,128)(2,1)S(1)} %bitcast_select_fusion.refs_5_, bf16[256,2304]{1,0:T(8,128)(2,1)S(1)} %get-tuple-element.88), kind=kOutput, calls=%fused_computation.1 | convolution fusion | flops 1210318848 | bytes 6422528 | tf_op jit(solution)/shard_map/dot_general | solution.py:19
  181.0 134.7 %mixer_backward.1 = (f32[64,4608]{1,0:T(8,128)}, f32[64,2304]{1,0:T(8,128)}, f32[64,512]{1,0:T(8,128)}, f32[64,1536]{1,0:T(8,128)}, bf16[128,1024]{1,0:T(8,128)(2,1)}, /*index=5*/f32[8,1024]{1,0:T(8,128)}) custom-call(bf16[4,2,2,64,4608]{4,3,2,1,0:T(8,128)(2,1)} %bitcast.57, bf16[4,2,2,64,2304]{4,3,2,1,0:T(8,128)(2,1)} %bitcast.58, ...), custom_call_target="tpu_custom_call" | custom-call | tf_op jit(solution)/shard_map/mixer_backward/pallas_call | solution.py:702
  315.8 1.9 copy.41
  317.7 3.1 reshape.221
  320.8 1.3 constant_dynamic-slice_fusion
  322.1 1.3 constant_dynamic-slice_fusion.2
  323.5 0.8 select_convert_fusion
  324.3 0.7 copy.49
  325.0 1.6 copy.50
  326.5 0.8 copy.51
  (68 shorter events, 4.8 us)
Async XLA Ops:
  0.6 8.0 %collective-permute-start = (bf16[2,32]{1,0:T(2,128)(2,1)}, bf16[2,32]{1,0:T(2,128)(2,1)S(1)}, u32[]{:S(2)}, u32[]{:S(2)}) collective-permute-start(bf16[2,32]{1,0:T(2,128)(2,1)} %param.18), channel_id=1, source_target_pairs={{0,1},{1,0},{2,3},{3,2},{4,5},{5,4},{6,7},{7,6},{8,9},{9,8},{10,11... | collective-permute-start | bytes 392 | tf_op jit(solution)/shard_map/ppermute | solution.py:754
  10.9 0.6 copy-start.11
  133.2 5.5 %copy-start.6 = (bf16[256,512]{1,0:T(8,128)(2,1)}, bf16[256,512]{1,0:T(8,128)(2,1)S(1)}, u32[]{:S(2)}) copy-start(bf16[256,512]{1,0:T(8,128)(2,1)S(1)} %multiply_convert_fusion.5.refs_13_) | copy-start | bytes 786436
  133.2 3.4 %collective-permute-start.1 = (bf16[2,512]{1,0:T(2,128)(2,1)S(1)}, bf16[2,512]{1,0:T(2,128)(2,1)S(1)}, u32[]{:S(2)}, u32[]{:S(2)}) collective-permute-start(bf16[2,512]{1,0:T(2,128)(2,1)S(1)} %constant_dynamic-slice_fusion.1), channel_id=1, source_target_pairs={{0,2},{2,4},{4,6},{6,8},{8,10},{10,12},{12,14},{14,16},{16,18},{18... | collective-permute-start | bytes 6152 | tf_op jit(solution)/shard_map/ppermute | solution.py:43
  136.7 2.0 copy-start.4
  138.7 4.6 %copy-start.7 = (bf16[256,512]{1,0:T(8,128)(2,1)}, bf16[256,512]{1,0:T(8,128)(2,1)S(1)}, u32[]{:S(2)}) copy-start(bf16[256,512]{1,0:T(8,128)(2,1)S(1)} %get-tuple-element.84.refs_8_) | copy-start | bytes 786436
  138.7 4.4 %copy-start.8 = (bf16[2,128,1024]{2,1,0:T(8,128)(2,1)S(1)}, bf16[2,128,1024]{2,1,0:T(8,128)(2,1)}, u32[]{:S(2)}) copy-start(bf16[2,128,1024]{2,1,0:T(8,128)(2,1)} %get-tuple-element.51) | copy-start | bytes 1572868
  138.7 15.6 %copy-start.2 = (bf16[2,128,1024]{2,1,0:T(8,128)(2,1)S(1)}, bf16[2,128,1024]{2,1,0:T(8,128)(2,1)}, u32[]{:S(2)}) copy-start(bf16[2,128,1024]{2,1,0:T(8,128)(2,1)} %get-tuple-element.45) | copy-start | bytes 1572868
  140.1 14.2 %copy-start.5 = (f32[256,1024]{1,0:T(8,128)S(1)}, f32[256,1024]{1,0:T(8,128)}, u32[]{:S(2)}) copy-start(f32[256,1024]{1,0:T(8,128)} %get-tuple-element.107) | copy-start | bytes 3145732
  140.1 14.2 %collective-permute-start.2 = (bf16[256,1024]{1,0:T(8,128)(2,1)S(1)}, bf16[256,1024]{1,0:T(8,128)(2,1)S(1)}, u32[]{:S(2)}, u32[]{:S(2)}) collective-permute-start(bf16[256,1024]{1,0:T(8,128)(2,1)S(1)} %get-tuple-element.106), channel_id=1, source_target_pairs={{0,1},{1,0},{2,3},{3,2},{4,5},{5,4},{6,7},{7,6},{8,9},{9,8},{10,11... | collective-permute-start | bytes 1572872 | tf_op jit(solution)/shard_map/ppermute | solution.py:764
  143.1 34.2 %copy-start.3 = (bf16[256,1024]{1,0:T(8,128)(2,1)}, bf16[256,1024]{1,0:T(8,128)(2,1)S(1)}, u32[]{:S(2)}) copy-start(bf16[256,1024]{1,0:T(8,128)(2,1)S(1)} %bitcast_select_fusion.refs_5_) | copy-start | bytes 1572868
  154.3 7.4 %slice-start.3 = ((s8[4718592]{0:T(1024)(128)(4,1)}), s8[4194304]{0:T(1024)(128)(4,1)S(1)}, s32[]{:S(2)}) async-start(s8[4718592]{0:T(1024)(128)(4,1)} %bitcast.87), calls=%async_computation.3 | async-start | bytes 8388608
  155.6 11.9 %copy-start = (f32[256,1024]{1,0:T(8,128)}, f32[256,1024]{1,0:T(8,128)S(1)}, u32[]{:S(2)}) copy-start(f32[256,1024]{1,0:T(8,128)S(1)} %get-tuple-element.83.refs_4_) | copy-start | bytes 3145732
  155.6 6.1 %slice-start.4 = ((s8[4718592]{0:T(1024)(128)(4,1)}), s8[524288]{0:T(1024)(128)(4,1)S(1)}, s32[]{:S(2)}) async-start(s8[4718592]{0:T(1024)(128)(4,1)} %bitcast.87), calls=%async_computation.4 | async-start | bytes 1048576
  155.6 8.0 %slice-start = ((s8[9437184]{0:T(1024)(128)(4,1)}), s8[4194304]{0:T(1024)(128)(4,1)S(1)}, s32[]{:S(2)}) async-start(s8[9437184]{0:T(1024)(128)(4,1)} %bitcast.83), calls=%async_computation | async-start | bytes 8388608
  155.6 8.0 %slice-start.1 = ((s8[9437184]{0:T(1024)(128)(4,1)}), s8[4194304]{0:T(1024)(128)(4,1)S(1)}, s32[]{:S(2)}) async-start(s8[9437184]{0:T(1024)(128)(4,1)} %bitcast.83), calls=%async_computation.1 | async-start | bytes 8388608
  161.7 1.9 slice-start.2
  176.7 146.7 %collective-permute-start.3 = (bf16[128,1024]{1,0:T(8,128)(2,1)S(1)}, bf16[128,1024]{1,0:T(8,128)(2,1)S(1)}, u32[]{:S(2)}, u32[]{:S(2)}) collective-permute-start(bf16[128,1024]{1,0:T(8,128)(2,1)S(1)} %dynamic-slice_convert_fusion), channel_id=1, source_target_pairs={{0,1},{1,0},{2,3},{3,2},{4,5},{5,4},{6,7},{7,6},{8,9},{9,8},{10,11... | collective-permute-start | bytes 786440 | tf_op jit(solution)/shard_map/ppermute | solution.py:773
  315.8 7.7 %copy-start.1 = (f32[256,1024]{1,0:T(8,128)S(1)}, f32[256,1024]{1,0:T(8,128)}, u32[]{:S(2)}) copy-start(f32[256,1024]{1,0:T(8,128)} %copy-done) | copy-start | bytes 3145732
  315.8 8.5 %copy-start.10 = (bf16[128,1024]{1,0:T(8,128)(2,1)S(1)}, bf16[128,1024]{1,0:T(8,128)(2,1)}, u32[]{:S(2)}) copy-start(bf16[128,1024]{1,0:T(8,128)(2,1)} %get-tuple-element.121) | copy-start | bytes 786436
  317.7 8.9 %copy-start.9 = (f32[64,2304]{1,0:T(8,128)S(1)}, f32[64,2304]{1,0:T(8,128)}, u32[]{:S(2)}) copy-start(f32[64,2304]{1,0:T(8,128)} %get-tuple-element.57) | copy-start | bytes 1769476

commit v4 on v3

--- a/solution.py
+++ b/solution.py
@@ -43,10 +43,11 @@
     return lax.ppermute(value, axis, [(source, source + steps) for source in range(leading, last)])
 
 
-def pieces_of(widths, size):
+def pieces_of(widths, size, fine=None):
     pieces = []
     for place, width in enumerate(widths):
-        step = size if width % size == 0 else width
+        step = size // 2 if place == fine else size
+        step = step if width % step == 0 else width
         pieces.extend((place, start, step) for start in range(0, width, step))
     return pieces
 
@@ -240,7 +241,7 @@
 
 def gather_all(shards, row_parts, seq, wide):
     tall = seq // (DEPTH * CORES)
-    pieces = pieces_of([shard.shape[1] for shard in shards], 768)
+    pieces = pieces_of([shard.shape[1] for shard in shards], 768, len(shards) - 1)
     count = len(pieces)
     moved = sum(shard.size * shard.dtype.itemsize for shard in shards) * seq
     dma = pltpu.SemaphoreType.DMA
@@ -690,7 +691,7 @@
     depth = width // seq
     bf, fl = jnp.bfloat16, jnp.float32
     widths = [term_gu.shape[1], term_down.shape[1], chans, 3 * chans]
-    pieces = pieces_of(widths, 768)
+    pieces = pieces_of(widths, 768, len(widths) - 1)
     ready = sum(1 for piece in pieces if piece[0] < 2)
     count = len(pieces)
     lead = (DEPTH, tall)

time: 328 us -> 325 us (level)
  no operation moved by 1% of the time
where the time goes in v4:
time: 325 us; the launch traced here: 324 us
  Pallas kernels  247 us (76%)
  matrix products  28.9 us (9%)
  local copies, waits for them, and re-layouts  19.1 us (6%)
  waiting for transfers between devices  12 us (4%)
  other arithmetic  9.21 us (3%)
  starting transfers between devices  6.5 us (2%)
    pallas_call x1, Pallas kernels, mixer_back(): pl.pallas_call(functools.partial(mixer_back_kernel, pieces, ready), out_s...  132 us
    pallas_call x1, Pallas kernels, gather_all(): pl.pallas_call(functools.partial(gather_kernel, pieces, len(shards), halv...  115 us
    ppermute x1, waiting for transfers between devices, mp_sum(): other = lax.ppermute(value.astype(jnp.bfloat16), 'mp', [(0, 1), (1, 0)])  11.5 us
    dot_general x2, matrix products, contract_rows(): lax.dot_general(left, right, (((0,), (0,)), ((), ())), preferred_element_...  9.1 us
    dot_general x3, matrix products, contract_cols(): lax.dot_general(left, right, (((1,), (1,)), ((), ())), preferred_element_...  8.99 us
  transfers between devices with their start and end apart: 4, of which 2 were waited for; matrix products, arithmetic and copies ran while one was open for 6% of the time, Pallas kernels for 41%

profile of v4, /device:TPU:0, one launch (start us, length us, event | category | flops | bytes accessed | tf_op | source)
XLA Modules:
  0.0 324.5 jit_solution(12771023493843092094)
XLA Ops:
  0.6 3.0 collective-permute-start
  4.3 0.7 compare_convert_fusion.3
  5.0 1.6 copy.36
  6.6 1.9 copy.37
  9.3 1.5 scatter.9.refs_0_
  11.5 115.2 %gather_weights.1 = (bf16[4,2,2,16,128]{4,3,2,1,0:T(8,128)(2,1)}, bf16[4,2,2,64,1536]{4,3,2,1,0:T(8,128)(2,1)}, bf16[4,2,2,64,512]{4,3,2,1,0:T(8,128)(2,1)}, bf1...) custom-call(bf16[16,128]{1,0:T(8,128)(2,1)} %copy-done.11, ...), custom_call_target="tpu_custom_call" | custom-call | bytes 294649856 | tf_op jit(solution)/shard_map/gather_weights/pallas_call | solution.py:249
  126.7 0.9 bitcast_convert_fusion
  127.5 1.2 fusion.4
  128.9 1.2 fusion.6
  130.1 2.9 fusion.21
  133.1 2.6 collective-permute-start.1
  136.6 2.0 multiply_convert_fusion.4
  138.6 1.4 fusion.19
  140.6 0.8 copy.31.refs_16_
  142.1 0.7 reshape.219.refs_20_
  143.1 11.5 %collective-permute-done.2 = bf16[256,1024]{1,0:T(8,128)(2,1)S(1)} collective-permute-done((bf16[256,1024]{1,0:T(8,128)(2,1)S(1)}, bf16[256,1024]{1,0:T(8,128)(2,1)S(1)}, u32[]{:S(2)}, u32[]{:S(2)}) %collective-permute-start.2) | collective-permute-done | bytes 524320 | tf_op jit(solution)/shard_map/ppermute | solution.py:765
  154.6 1.3 multiply_reduce_fusion
  156.0 6.0 %fusion.16 = f32[256,4608]{1,0:T(8,128)S(1)} fusion(bf16[1024,4608]{1,0:T(8,128)(2,1)} %bitcast.82, f32[256,1024]{1,0:T(8,128)S(1)} %get-tuple-element.83.refs_4_, f32[1024]{0:T(1024)S(1)} %mul.168, f32[256]{0:T(256)S(1)} %add_rsqrt_fusion), kind=kOutput, calls=%fused_computation.57 | convolution fusion | flops 2416705536 | bytes 15209472 | tf_op jit(solution)/shard_map/dot_general | solution.py:845
  162.1 1.9 multiply_convert_fusion.1
  164.0 3.8 %fusion.20 = (bf16[256,1024]{1,0:T(8,128)(2,1)}, f32[256,1024]{1,0:T(8,128)}) fusion(bf16[1024,4608]{1,0:T(8,128)(2,1)S(1)} %bitcast.85, bf16[256,2304]{1,0:T(8,128)(2,1)S(1)} %get-tuple-element.87, bf16[256,2304]{1,0:T(8,128)(2,1)S(1)} %get-tuple-element.86), kind=kOutput, calls=%fused_computation.61 | convolution fusion | flops 2420899840 | bytes 13369344 | tf_op jit(solution)/shard_map/dot_general | solution.py:25
  167.8 5.4 %convolution_convert_fusion = bf16[1024,4608]{1,0:T(8,128)(2,1)} fusion(bf16[256,2304]{1,0:T(8,128)(2,1)S(1)} %get-tuple-element.87, bf16[256,2304]{1,0:T(8,128)(2,1)S(1)} %get-tuple-element.86, f32[256,1024]{1,0:T(8,128)S(1)} %get-tuple-element.83.refs_4_, f32[1024]{0:T(1024)S(1)} %mul.168, f32[256]{0:T(256)S(1)} %add_rsqrt_fusion), kind=kOutput, calls=%fused_computation | convolution fusion | flops 2426142720 | bytes 12850176 | tf_op jit(solution)/shard_map/dot_general | solution.py:19
  173.2 3.7 %fusion.22 = f32[256,1024]{1,0:T(8,128)S(1)} fusion(bf16[256,2304]{1,0:T(8,128)(2,1)S(1)} %get-tuple-element.88, bf16[1024,2304]{1,0:T(8,128)(2,1)} %bitcast.86), kind=kOutput, calls=%fused_computation.63 | convolution fusion | flops 1207959552 | bytes 6946816 | tf_op jit(solution)/shard_map/dot_general | solution.py:25
  177.4 3.7 %convolution_convert_fusion.1 = bf16[1024,2304]{1,0:T(8,128)(2,1)} fusion(bf16[256,1024]{1,0:T(8,128)(2,1)S(1)} %bitcast_select_fusion.refs_5_, bf16[256,2304]{1,0:T(8,128)(2,1)S(1)} %get-tuple-element.88), kind=kOutput, calls=%fused_computation.1 | convolution fusion | flops 1210318848 | bytes 6422528 | tf_op jit(solution)/shard_map/dot_general | solution.py:19
  181.1 131.8 %mixer_backward.1 = (f32[64,4608]{1,0:T(8,128)}, f32[64,2304]{1,0:T(8,128)}, f32[64,512]{1,0:T(8,128)}, f32[64,1536]{1,0:T(8,128)}, bf16[128,1024]{1,0:T(8,128)(2,1)}, /*index=5*/f32[8,1024]{1,0:T(8,128)}) custom-call(bf16[4,2,2,64,4608]{4,3,2,1,0:T(8,128)(2,1)} %bitcast.57, bf16[4,2,2,64,2304]{4,3,2,1,0:T(8,128)(2,1)} %bitcast.58, ...), custom_call_target="tpu_custom_call" | custom-call | tf_op jit(solution)/shard_map/mixer_backward/pallas_call | solution.py:703
  312.9 1.9 copy.41
  314.8 3.1 reshape.221
  317.9 1.3 constant_dynamic-slice_fusion
  319.2 1.3 constant_dynamic-slice_fusion.2
  320.6 0.8 select_convert_fusion
  321.4 0.7 copy.49
  322.1 1.6 copy.50
  323.6 0.8 copy.51
  (68 shorter events, 4.4 us)
Async XLA Ops:
  0.6 8.0 %collective-permute-start = (bf16[2,32]{1,0:T(2,128)(2,1)}, bf16[2,32]{1,0:T(2,128)(2,1)S(1)}, u32[]{:S(2)}, u32[]{:S(2)}) collective-permute-start(bf16[2,32]{1,0:T(2,128)(2,1)} %param.18), channel_id=1, source_target_pairs={{0,1},{1,0},{2,3},{3,2},{4,5},{5,4},{6,7},{7,6},{8,9},{9,8},{10,11... | collective-permute-start | bytes 392 | tf_op jit(solution)/shard_map/ppermute | solution.py:755
  10.9 0.6 copy-start.11
  133.1 5.5 %copy-start.6 = (bf16[256,512]{1,0:T(8,128)(2,1)}, bf16[256,512]{1,0:T(8,128)(2,1)S(1)}, u32[]{:S(2)}) copy-start(bf16[256,512]{1,0:T(8,128)(2,1)S(1)} %multiply_convert_fusion.5.refs_13_) | copy-start | bytes 786436
  133.1 3.4 %collective-permute-start.1 = (bf16[2,512]{1,0:T(2,128)(2,1)S(1)}, bf16[2,512]{1,0:T(2,128)(2,1)S(1)}, u32[]{:S(2)}, u32[]{:S(2)}) collective-permute-start(bf16[2,512]{1,0:T(2,128)(2,1)S(1)} %constant_dynamic-slice_fusion.1), channel_id=1, source_target_pairs={{0,2},{2,4},{4,6},{6,8},{8,10},{10,12},{12,14},{14,16},{16,18},{18... | collective-permute-start | bytes 6152 | tf_op jit(solution)/shard_map/ppermute | solution.py:43
  136.6 2.0 copy-start.4
  138.6 4.5 %copy-start.7 = (bf16[256,512]{1,0:T(8,128)(2,1)}, bf16[256,512]{1,0:T(8,128)(2,1)S(1)}, u32[]{:S(2)}) copy-start(bf16[256,512]{1,0:T(8,128)(2,1)S(1)} %get-tuple-element.84.refs_8_) | copy-start | bytes 786436
  138.6 4.3 %copy-start.8 = (bf16[2,128,1024]{2,1,0:T(8,128)(2,1)S(1)}, bf16[2,128,1024]{2,1,0:T(8,128)(2,1)}, u32[]{:S(2)}) copy-start(bf16[2,128,1024]{2,1,0:T(8,128)(2,1)} %get-tuple-element.51) | copy-start | bytes 1572868
  138.6 16.0 %copy-start.2 = (bf16[2,128,1024]{2,1,0:T(8,128)(2,1)S(1)}, bf16[2,128,1024]{2,1,0:T(8,128)(2,1)}, u32[]{:S(2)}) copy-start(bf16[2,128,1024]{2,1,0:T(8,128)(2,1)} %get-tuple-element.45) | copy-start | bytes 1572868
  140.1 14.6 %copy-start.5 = (f32[256,1024]{1,0:T(8,128)S(1)}, f32[256,1024]{1,0:T(8,128)}, u32[]{:S(2)}) copy-start(f32[256,1024]{1,0:T(8,128)} %get-tuple-element.107) | copy-start | bytes 3145732
  140.1 14.6 %collective-permute-start.2 = (bf16[256,1024]{1,0:T(8,128)(2,1)S(1)}, bf16[256,1024]{1,0:T(8,128)(2,1)S(1)}, u32[]{:S(2)}, u32[]{:S(2)}) collective-permute-start(bf16[256,1024]{1,0:T(8,128)(2,1)S(1)} %get-tuple-element.106), channel_id=1, source_target_pairs={{0,1},{1,0},{2,3},{3,2},{4,5},{5,4},{6,7},{7,6},{8,9},{9,8},{10,11... | collective-permute-start | bytes 1572872 | tf_op jit(solution)/shard_map/ppermute | solution.py:765
  143.0 34.4 %copy-start.3 = (bf16[256,1024]{1,0:T(8,128)(2,1)}, bf16[256,1024]{1,0:T(8,128)(2,1)S(1)}, u32[]{:S(2)}) copy-start(bf16[256,1024]{1,0:T(8,128)(2,1)S(1)} %bitcast_select_fusion.refs_5_) | copy-start | bytes 1572868
  154.6 7.4 %slice-start.3 = ((s8[4718592]{0:T(1024)(128)(4,1)}), s8[4194304]{0:T(1024)(128)(4,1)S(1)}, s32[]{:S(2)}) async-start(s8[4718592]{0:T(1024)(128)(4,1)} %bitcast.87), calls=%async_computation.3 | async-start | bytes 8388608
  155.9 11.9 %copy-start = (f32[256,1024]{1,0:T(8,128)}, f32[256,1024]{1,0:T(8,128)S(1)}, u32[]{:S(2)}) copy-start(f32[256,1024]{1,0:T(8,128)S(1)} %get-tuple-element.83.refs_4_) | copy-start | bytes 3145732
  156.0 6.1 %slice-start.4 = ((s8[4718592]{0:T(1024)(128)(4,1)}), s8[524288]{0:T(1024)(128)(4,1)S(1)}, s32[]{:S(2)}) async-start(s8[4718592]{0:T(1024)(128)(4,1)} %bitcast.87), calls=%async_computation.4 | async-start | bytes 1048576
  156.0 8.0 %slice-start = ((s8[9437184]{0:T(1024)(128)(4,1)}), s8[4194304]{0:T(1024)(128)(4,1)S(1)}, s32[]{:S(2)}) async-start(s8[9437184]{0:T(1024)(128)(4,1)} %bitcast.83), calls=%async_computation | async-start | bytes 8388608
  156.0 8.0 %slice-start.1 = ((s8[9437184]{0:T(1024)(128)(4,1)}), s8[4194304]{0:T(1024)(128)(4,1)S(1)}, s32[]{:S(2)}) async-start(s8[9437184]{0:T(1024)(128)(4,1)} %bitcast.83), calls=%async_computation.1 | async-start | bytes 8388608
  162.1 1.9 slice-start.2
  177.0 143.5 %collective-permute-start.3 = (bf16[128,1024]{1,0:T(8,128)(2,1)S(1)}, bf16[128,1024]{1,0:T(8,128)(2,1)S(1)}, u32[]{:S(2)}, u32[]{:S(2)}) collective-permute-start(bf16[128,1024]{1,0:T(8,128)(2,1)S(1)} %dynamic-slice_convert_fusion), channel_id=1, source_target_pairs={{0,1},{1,0},{2,3},{3,2},{4,5},{5,4},{6,7},{7,6},{8,9},{9,8},{10,11... | collective-permute-start | bytes 786440 | tf_op jit(solution)/shard_map/ppermute | solution.py:774
  312.9 7.7 %copy-start.1 = (f32[256,1024]{1,0:T(8,128)S(1)}, f32[256,1024]{1,0:T(8,128)}, u32[]{:S(2)}) copy-start(f32[256,1024]{1,0:T(8,128)} %copy-done) | copy-start | bytes 3145732
  312.9 8.5 %copy-start.10 = (bf16[128,1024]{1,0:T(8,128)(2,1)S(1)}, bf16[128,1024]{1,0:T(8,128)(2,1)}, u32[]{:S(2)}) copy-start(bf16[128,1024]{1,0:T(8,128)(2,1)} %get-tuple-element.121) | copy-start | bytes 786436
  314.8 8.9 %copy-start.9 = (f32[64,2304]{1,0:T(8,128)S(1)}, f32[64,2304]{1,0:T(8,128)}, u32[]{:S(2)}) copy-start(f32[64,2304]{1,0:T(8,128)} %get-tuple-element.57) | copy-start | bytes 1769476
